TPU v7x, 128 devices: a whole 4x4x4 slice. The times are simulated.
128 devices in a mesh: slab: 16 (over x_lo, y, core), angle: 8 (over z, x_hi).
Axes of the slice: x: 4 (x_hi: 2, x_lo: 2; x = x_hi * 2 + x_lo), y: 4, z: 4, core: 2. Of those that a mesh axis runs over, the one named last changes fastest.
Arguments:
- fields: float32 [8, 2, 2, 3, 64, 128, 128], P('angle', None, None, None, 'slab'), may hold values from -6 to 6
- spectra: float32 [8, 2, 2, 3, 64, 128, 128], P('angle', None, None, None, 'slab'), may hold values from -6 to 6
- inv_eps: float32 [64, 128, 128], P('slab'), may hold values from 0.15 to 1
- step_phase: float32 [2], replicated, may hold values from -3.140625 to 3.140625
Outputs:
- fields_out: float32 [8, 2, 2, 3, 64, 128, 128], P('angle', None, None, None, 'slab')
- spectra_out: float32 [8, 2, 2, 3, 64, 128, 128], P('angle', None, None, None, 'slab')
- gradient: float32 [8, 128, 128], P(None, 'slab')
All inputs are finite; a program needn't handle non-finite values.
Results may differ from a plain program's by a relative error of at most 0.00007.
Values sent between devices are 32-bit elements; how exact they have to be, the bound alone decides.
A program may use at most 64 MiB of HBM per device.

v0:
```python
import jax
import jax.numpy as jnp
from jax import lax
from jax.sharding import PartitionSpec as P

DZ = 8
STEPS = 2


COURANT = 0.5
FILTER_TAPS = (0.0625, 0.25, 0.375, 0.25, 0.0625)


def padded_2(block, sides, width):
    for axis, dim in sides:
        count = lax.axis_size(axis)
        forward = [(i, i + 1) for i in range(count - 1)]
        backward = [(target, source) for source, target in forward]
        low = lax.ppermute(
            lax.slice_in_dim(block, block.shape[dim] - width, None, axis=dim), axis, forward
        )
        high = lax.ppermute(lax.slice_in_dim(block, 0, width, axis=dim), axis, backward)
        block = jnp.concatenate([low, block, high], axis=dim)
    return block


def from_behind(block, axis, distance):
    devices = range(lax.axis_size(axis))
    route = [(i - distance, i) for i in devices if i - distance in devices]
    return lax.ppermute(block, axis, route)


def ahead_diff(array_in, along_axis):
    length = array_in.shape[along_axis]
    shifted = jnp.concatenate(
        [
            lax.slice_in_dim(array_in, 1, length, axis=along_axis),
            jnp.zeros_like(lax.slice_in_dim(array_in, 0, 1, axis=along_axis)),
        ],
        axis=along_axis,
    )
    return shifted - array_in


def behind_diff(array_in, along_axis):
    length = array_in.shape[along_axis]
    shifted = jnp.concatenate(
        [
            jnp.zeros_like(lax.slice_in_dim(array_in, 0, 1, axis=along_axis)),
            lax.slice_in_dim(array_in, 0, length - 1, axis=along_axis),
        ],
        axis=along_axis,
    )
    return array_in - shifted


def curl_ahead(e_field, ahead_planes):
    ahead_xy = (
        jnp.concatenate([e_field[:, 0:2, 1:], ahead_planes[:, :, None]], axis=2) - e_field[:, 0:2]
    )
    curl_x = ahead_diff(e_field[:, 2], 3) - ahead_xy[:, 1]
    curl_y = ahead_xy[:, 0] - ahead_diff(e_field[:, 2], 2)
    curl_z = ahead_diff(e_field[:, 1], 2) - ahead_diff(e_field[:, 0], 3)
    return jnp.stack([curl_x, curl_y, curl_z], axis=1)


def curl_behind(h_field, behind_planes):
    behind_xy = h_field[:, 0:2] - jnp.concatenate(
        [behind_planes[:, :, None], h_field[:, 0:2, :-1]], axis=2
    )
    curl_x = behind_diff(h_field[:, 2], 3) - behind_xy[:, 1]
    curl_y = behind_xy[:, 0] - behind_diff(h_field[:, 2], 2)
    curl_z = behind_diff(h_field[:, 1], 2) - behind_diff(h_field[:, 0], 3)
    return jnp.stack([curl_x, curl_y, curl_z], axis=1)


def smooth_owned(owned_block):
    columns = owned_block.shape[1]
    widened = padded_2(owned_block, (("slab", 1),), 2)
    along_x = FILTER_TAPS[0] * widened[:, 0:columns]
    for offset in range(1, 5):
        along_x = along_x + FILTER_TAPS[offset] * widened[:, offset : offset + columns]
    rows_y = along_x.shape[2]
    padded = jnp.pad(along_x, ((0, 0), (0, 0), (2, 2)))
    along_y = FILTER_TAPS[0] * padded[:, :, 0:rows_y]
    for offset in range(1, 5):
        along_y = along_y + FILTER_TAPS[offset] * padded[:, :, offset : offset + rows_y]
    return along_y


def per_device(fields, spectra, inv_eps, step_phase):
    e_field = fields[0, :, 0]
    h_field = fields[0, :, 1]
    re_part = spectra[0, :, 0]
    im_part = spectra[0, :, 1]
    for step_index in range(STEPS):
        ahead_planes = from_behind(e_field[:, 0:2, 0], "slab", -1)
        h_field = h_field - COURANT * curl_ahead(e_field, ahead_planes)
        behind_planes = from_behind(h_field[:, 0:2, -1], "slab", 1)
        e_field = e_field + COURANT * inv_eps * curl_behind(h_field, behind_planes)
        re_part = re_part + e_field * jnp.cos(step_phase[step_index])
        im_part = im_part + e_field * jnp.sin(step_phase[step_index])
    fields_out = jnp.stack([e_field, h_field], axis=1)[None]
    spectra_out = jnp.stack([re_part, im_part], axis=1)[None]
    density = jnp.sum(re_part[0] * re_part[1] - im_part[0] * im_part[1], axis=0)
    local_planes = density.shape[0]
    all_planes = local_planes * lax.axis_size("slab")
    slab_index = lax.axis_index("slab")
    planes = slab_index * local_planes + jnp.arange(local_planes, dtype=jnp.int32)
    wanted = (all_planes - DZ) // 2 + jnp.arange(DZ, dtype=jnp.int32)
    selector = (wanted[:, None] == planes[None, :]).astype(jnp.float32)
    design_slab = jnp.einsum("dk,kxy->dxy", selector, density, precision=lax.Precision.HIGHEST)
    design_slab = lax.psum(design_slab, "angle")
    even_slab = 0.5 * (design_slab + design_slab[:, ::-1, :])
    owned_even = lax.psum_scatter(even_slab, "slab", scatter_dimension=1, tiled=True)
    result = smooth_owned(owned_even)
    gradient = result * (1.0 / lax.axis_size("angle"))
    return (fields_out, spectra_out, gradient)


def solution(mesh):
    in_specs = (
        P("angle", None, None, None, "slab", None, None),
        P("angle", None, None, None, "slab", None, None),
        P("slab", None, None),
        P(),
    )
    out_specs = (
        P("angle", None, None, None, "slab", None, None),
        P("angle", None, None, None, "slab", None, None),
        P(None, "slab", None),
    )
    return jax.shard_map(
        per_device, mesh=mesh, in_specs=in_specs, out_specs=out_specs, check_vma=False
    )
```

profile of v0, /device:TPU:1, one launch (start us, length us, event | category | flops | bytes accessed | tf_op | source)
XLA Modules:
  0.0 222.6 jit_solution(12116787620977879856)
XLA Ops:
  7.2 1.5 copy_bitcast_fusion
  8.7 0.7 slice_bitcast_fusion.21
  9.5 3.6 %collective-permute-start = (f32[2,2,128,128]{3,2,0,1:T(8,128)}, f32[2,2,128,128]{3,2,0,1:T(8,128)}, u32[]{:S(2)}, u32[]{:S(2)}) collective-permute-start(f32[2,2,128,128]{3,2,0,1:T(8,128)} %slice_bitcast_fusion.21), channel_id=1, source_target_pairs={{8,0},{16,8},{24,16},{32,24},{40,32},{48,40},{56,48},{64,56},{72,6... | collective-permute-start | bytes 786440 | tf_op jit(solution)/shard_map/ppermute | solution.py:30
  13.0 1.2 slice_bitcast_fusion.19
  14.2 0.7 fusion.59
  14.9 1.3 fusion.57
  16.3 1.3 copy-done.11
  17.7 0.2 slice.284
  21.0 0.2 slice.294
  21.2 1.1 slice_subtract_fusion.1
  22.3 1.4 fusion.39
  23.7 0.9 copy-done
  24.6 0.3 bitcast_subtract_fusion.1
  24.9 3.2 %collective-permute-start.1 = (f32[2,2,128,128]{3,2,0,1:T(8,128)S(1)}, f32[2,2,128,128]{3,2,0,1:T(8,128)S(1)}, u32[]{:S(2)}, u32[]{:S(2)}) collective-permute-start(f32[2,2,128,128]{3,2,0,1:T(8,128)S(1)} %copy_bitcast_fusion.2), channel_id=1, source_target_pairs={{0,8},{8,16},{16,24},{24,32},{32,40},{40,48},{48,56},{56,64},{64,7... | collective-permute-start | bytes 786440 | tf_op jit(solution)/shard_map/ppermute | solution.py:30
  28.2 3.1 %collective-permute-done.1 = f32[2,2,128,128]{3,2,0,1:T(8,128)S(1)} collective-permute-done((f32[2,2,128,128]{3,2,0,1:T(8,128)S(1)}, f32[2,2,128,128]{3,2,0,1:T(8,128)S(1)}, u32[]{:S(2)}, u32[]{:S(2)}) %collective-permute-start.1) | collective-permute-done | bytes 262176 | tf_op jit(solution)/shard_map/ppermute | solution.py:30
  31.5 1.4 fusion.44
  32.9 0.2 fusion.1
  33.2 1.9 collective-permute-start.2
  35.3 0.2 slice.308
  35.6 0.2 slice.318
  35.8 5.9 %collective-permute-done.2 = f32[2,2,128,128]{3,2,0,1:T(8,128)S(1)} collective-permute-done((f32[2,2,128,128]{3,2,0,1:T(8,128)S(1)}, f32[2,2,128,128]{3,2,0,1:T(8,128)S(1)}, u32[]{:S(2)}, u32[]{:S(2)}) %collective-permute-start.2) | collective-permute-done | bytes 262176 | tf_op jit(solution)/shard_map/ppermute | solution.py:30
  41.8 1.4 fusion.48
  43.1 0.3 copy_subtract_fusion
  43.4 0.5 copy-done.10
  43.9 1.9 collective-permute-start.3
  45.9 0.1 slice_bitcast_fusion.4
  46.0 3.1 %collective-permute-done.3 = f32[2,2,128,128]{3,2,0,1:T(8,128)S(1)} collective-permute-done((f32[2,2,128,128]{3,2,0,1:T(8,128)S(1)}, f32[2,2,128,128]{3,2,0,1:T(8,128)S(1)}, u32[]{:S(2)}, u32[]{:S(2)}) %collective-permute-start.3) | collective-permute-done | bytes 262176 | tf_op jit(solution)/shard_map/ppermute | solution.py:30
  49.3 1.4 fusion.51
  50.8 1.0 fusion.6
  51.8 0.2 fusion.10
  52.0 1.5 fusion.20
  53.6 2.2 pad_maximum_fusion
  55.8 0.6 copy-done.1
  56.4 1.6 fusion.4
  57.9 83.8 %all-reduce.19.cloned.1.call-done = f32[8,128,128]{2,0,1:T(8,128)} async-done(((f32[8,128,128]{2,0,1:T(8,128)}), f32[8,128,128]{2,0,1:T(8,128)}) %all-reduce.19.cloned.1.call-update) | async-done | bytes 524304 | tf_op jit(solution)/shard_map/psum | solution.py:113
  141.7 2.1 fusion.11
  143.8 4.2 %fusion.8 = (f32[2,1,3,4,128,128]{5,4,3,0,2,1:T(8,128)}, f32[2,1,3,4,128,128]{5,4,3,0,2,1:T(8,128)S(1)}, f32[2,1,3,4,128,128]{5,4,3,0,2,1:T(8,128)S(1)}) fusion(f32[1,2,1,3,4,128,128]{6,5,4,3,2,1,0:T(8,128)} %get-tuple-element.22, f32[]{:T(128)} %bitcast.56, f32[]{:T(128)} %bitcast.55, f32[2,1,1,4,128,128]{5,4,3,0,2,1:T(8,128)} %bitcast.282, ...), kind=kLoop, calls=%fused_computation.24 | loop fusion | flops 4718592 | bytes 11272200 | tf_op jit(solution)/shard_map/add | solution.py:101
  148.1 1.9 maximum_bitcast_fusion
  149.9 0.2 copy-done.3
  150.1 0.4 fusion.7
  150.5 53.3 %reduce-scatter.2.cloned.1.call-done = f32[8,8,128]{2,0,1:T(8,128)} async-done(((f32[8,128,128]{2,0,1:T(8,128)}), f32[8,8,128]{2,0,1:T(8,128)}) %reduce-scatter.2.cloned.1.call-update) | async-done | bytes 32784 | tf_op jit(solution)/shard_map/reduce_scatter | solution.py:115
  203.8 0.7 fusion.58
  204.6 3.4 %collective-permute-start.4 = (f32[8,2,128]{2,0,1:T(8,128)S(1)}, f32[8,2,128]{2,0,1:T(8,128)S(1)}, u32[]{:S(2)}, u32[]{:S(2)}) collective-permute-start(f32[8,2,128]{2,0,1:T(8,128)S(1)} %get-tuple-element.61), channel_id=1, source_target_pairs={{0,8},{8,16},{16,24},{24,32},{32,40},{40,48},{48,56},{56,64},{64,7... | collective-permute-start | bytes 24584 | tf_op jit(solution)/shard_map/ppermute | solution.py:19
  208.0 0.2 maximum_bitcast_fusion.1
  208.2 1.9 copy.74
  210.1 4.1 %collective-permute-start.5 = (f32[8,2,128]{2,0,1:T(8,128)S(1)}, f32[8,2,128]{2,0,1:T(8,128)S(1)}, u32[]{:S(2)}, u32[]{:S(2)}) collective-permute-start(f32[8,2,128]{2,0,1:T(8,128)S(1)} %get-tuple-element.62), channel_id=1, source_target_pairs={{8,0},{16,8},{24,16},{32,24},{40,32},{48,40},{56,48},{64,56},{72,6... | collective-permute-start | bytes 24584 | tf_op jit(solution)/shard_map/ppermute | solution.py:22
  214.2 0.8 collective-permute-done.5
  215.1 0.6 copy.75
  (59 shorter events, 1.4 us)
Async XLA Ops:
  7.2 134.5 %all-reduce.19.cloned.1.call-start = ((), (), s32[]{:S(2)}) async-start(), calls=%async_computation.1 | async-start | bytes 1048576 | tf_op jit(solution)/shard_map/psum | solution.py:113
  9.4 4.8 %copy-start.17 = (f32[2]{0:T(128)S(1)}, f32[2]{0:T(128)}, u32[]{:S(2)}) copy-start(f32[2]{0:T(128)} %param.7) | copy-start | bytes 28
  9.5 5.5 %copy-start.12 = (f32[1,2,2,3,4,128,128]{6,5,4,3,2,1,0:T(8,128)S(1)}, f32[1,2,2,3,4,128,128]{6,5,4,3,2,1,0:T(8,128)}, u32[]{:S(2)}) copy-start(f32[1,2,2,3,4,128,128]{6,5,4,3,2,1,0:T(8,128)} %param.5) | copy-start | bytes 9437188
  9.5 11.8 %collective-permute-start = (f32[2,2,128,128]{3,2,0,1:T(8,128)}, f32[2,2,128,128]{3,2,0,1:T(8,128)}, u32[]{:S(2)}, u32[]{:S(2)}) collective-permute-start(f32[2,2,128,128]{3,2,0,1:T(8,128)} %slice_bitcast_fusion.21), channel_id=1, source_target_pairs={{8,0},{16,8},{24,16},{32,24},{40,32},{48,40},{56,48},{64,56},{72,6... | collective-permute-start | bytes 786440 | tf_op jit(solution)/shard_map/ppermute | solution.py:30
  16.3 34.4 %copy-start.2 = (f32[1,2,1,3,4,128,128]{6,5,4,3,2,1,0:T(8,128)}, f32[1,2,1,3,4,128,128]{6,5,4,3,2,1,0:T(8,128)S(1)}, u32[]{:S(2)}) copy-start(f32[1,2,1,3,4,128,128]{6,5,4,3,2,1,0:T(8,128)S(1)} %get-tuple-element.21) | copy-start | bytes 4718596
  16.3 1.4 copy-start.11
  16.3 4.7 %copy-start.14 = (f32[2,4,128,128]{3,2,1,0:T(8,128)S(1)}, f32[2,4,128,128]{3,2,1,0:T(8,128)}, u32[]{:S(2)}) copy-start(f32[2,4,128,128]{3,2,1,0:T(8,128)} %get-tuple-element.58) | copy-start | bytes 1572868
  17.7 3.3 %copy-start.13 = (f32[2,4,128,128]{3,2,1,0:T(8,128)S(1)}, f32[2,4,128,128]{3,2,1,0:T(8,128)}, u32[]{:S(2)}) copy-start(f32[2,4,128,128]{3,2,1,0:T(8,128)} %get-tuple-element.57) | copy-start | bytes 1572868
  17.9 3.3 %copy-start.15 = (f32[4,128,128]{2,1,0:T(8,128)S(1)}, f32[4,128,128]{2,1,0:T(8,128)}, u32[]{:S(2)}) copy-start(f32[4,128,128]{2,1,0:T(8,128)} %param.6) | copy-start | bytes 786436
  22.3 2.3 %copy-start = (f32[1,2,2,3,4,128,128]{6,5,4,3,2,1,0:T(8,128)S(1)}, f32[1,2,2,3,4,128,128]{6,5,4,3,2,1,0:T(8,128)}, u32[]{:S(2)}) copy-start(f32[1,2,2,3,4,128,128]{6,5,4,3,2,1,0:T(8,128)} %param.4) | copy-start | bytes 9437188
  23.7 7.8 %copy-start.8 = (f32[2,4,128,128]{3,2,1,0:T(8,128)}, f32[2,4,128,128]{3,2,1,0:T(8,128)S(1)}, u32[]{:S(2)}) copy-start(f32[2,4,128,128]{3,2,1,0:T(8,128)S(1)} %get-tuple-element.49) | copy-start | bytes 1572868
  24.9 6.5 %collective-permute-start.1 = (f32[2,2,128,128]{3,2,0,1:T(8,128)S(1)}, f32[2,2,128,128]{3,2,0,1:T(8,128)S(1)}, u32[]{:S(2)}, u32[]{:S(2)}) collective-permute-start(f32[2,2,128,128]{3,2,0,1:T(8,128)S(1)} %copy_bitcast_fusion.2), channel_id=1, source_target_pairs={{0,8},{8,16},{16,24},{24,32},{32,40},{40,48},{48,56},{56,64},{64,7... | collective-permute-start | bytes 786440 | tf_op jit(solution)/shard_map/ppermute | solution.py:30
  32.9 17.8 %copy-start.5 = (f32[2,4,128,128]{3,2,1,0:T(8,128)}, f32[2,4,128,128]{3,2,1,0:T(8,128)S(1)}, u32[]{:S(2)}) copy-start(f32[2,4,128,128]{3,2,1,0:T(8,128)S(1)} %get-tuple-element.44) | copy-start | bytes 1572868
  33.2 8.4 %collective-permute-start.2 = (f32[2,2,128,128]{3,2,0,1:T(8,128)S(1)}, f32[2,2,128,128]{3,2,0,1:T(8,128)S(1)}, u32[]{:S(2)}, u32[]{:S(2)}) collective-permute-start(f32[2,2,128,128]{3,2,0,1:T(8,128)S(1)} %slice_bitcast_fusion.20), channel_id=1, source_target_pairs={{8,0},{16,8},{24,16},{32,24},{40,32},{48,40},{56,48},{64,56},{72,6... | collective-permute-start | bytes 786440 | tf_op jit(solution)/shard_map/ppermute | solution.py:30
  43.1 0.8 copy-start.10
  43.9 5.2 %collective-permute-start.3 = (f32[2,2,128,128]{3,2,0,1:T(8,128)S(1)}, f32[2,2,128,128]{3,2,0,1:T(8,128)S(1)}, u32[]{:S(2)}, u32[]{:S(2)}) collective-permute-start(f32[2,2,128,128]{3,2,0,1:T(8,128)S(1)} %copy_bitcast_fusion.1), channel_id=1, source_target_pairs={{0,8},{8,16},{16,24},{24,32},{32,40},{40,48},{48,56},{56,64},{64,7... | collective-permute-start | bytes 786440 | tf_op jit(solution)/shard_map/ppermute | solution.py:30
  49.3 1.5 copy-start.4
  50.6 1.1 copy-start.9
  53.5 150.3 %reduce-scatter.2.cloned.1.call-start = ((), (), s32[]{:S(2)}) async-start(), calls=%async_computation.2 | async-start | bytes 557056 | tf_op jit(solution)/shard_map/reduce_scatter | solution.py:115
  53.5 2.8 %copy-start.1 = (f32[1,2,2,3,4,128,128]{6,5,4,3,2,1,0:T(8,128)S(1)}, f32[1,2,2,3,4,128,128]{6,5,4,3,2,1,0:T(8,128)}, u32[]{:S(2)}) copy-start(f32[1,2,2,3,4,128,128]{6,5,4,3,2,1,0:T(8,128)} %param.4) | copy-start | bytes 9437188
  143.8 4.3 %copy-start.6 = (f32[2,1,3,4,128,128]{5,4,3,2,1,0:T(8,128)S(1)}, f32[2,1,3,4,128,128]{5,4,3,2,1,0:T(8,128)}, u32[]{:S(2)}) copy-start(f32[2,1,3,4,128,128]{5,4,3,2,1,0:T(8,128)} %fusion.4) | copy-start | bytes 4718596
  148.1 2.0 copy-start.3
  150.1 57.9 %copy-start.7 = (f32[2,1,3,4,128,128]{5,4,3,0,2,1:T(8,128)S(1)}, f32[2,1,3,4,128,128]{5,4,3,0,2,1:T(8,128)}, u32[]{:S(2)}) copy-start(f32[2,1,3,4,128,128]{5,4,3,0,2,1:T(8,128)} %get-tuple-element.12) | copy-start | bytes 4718596
  204.6 9.6 %collective-permute-start.4 = (f32[8,2,128]{2,0,1:T(8,128)S(1)}, f32[8,2,128]{2,0,1:T(8,128)S(1)}, u32[]{:S(2)}, u32[]{:S(2)}) collective-permute-start(f32[8,2,128]{2,0,1:T(8,128)S(1)} %get-tuple-element.61), channel_id=1, source_target_pairs={{0,8},{8,16},{16,24},{24,32},{32,40},{40,48},{48,56},{56,64},{64,7... | collective-permute-start | bytes 24584 | tf_op jit(solution)/shard_map/ppermute | solution.py:19
  208.2 6.0 %copy-start.16 = (f32[8,8,128]{2,0,1:T(8,128)S(1)}, f32[8,8,128]{2,0,1:T(8,128)}, u32[]{:S(2)}) copy-start(f32[8,8,128]{2,0,1:T(8,128)} %reduce-scatter.2.cloned.1.call-done) | copy-start | bytes 98308
  210.1 5.0 %collective-permute-start.5 = (f32[8,2,128]{2,0,1:T(8,128)S(1)}, f32[8,2,128]{2,0,1:T(8,128)S(1)}, u32[]{:S(2)}, u32[]{:S(2)}) collective-permute-start(f32[8,2,128]{2,0,1:T(8,128)S(1)} %get-tuple-element.62), channel_id=1, source_target_pairs={{8,0},{16,8},{24,16},{32,24},{40,32},{48,40},{56,48},{64,56},{72,6... | collective-permute-start | bytes 24584 | tf_op jit(solution)/shard_map/ppermute | solution.py:22
Sparse Core Ops, SparseCore 0:
  53.6 88.0 all-reduce.18
  144.2 59.6 reduce-scatter.1
where the time goes:
time: 227 us; the launch traced here: 223 us
  waiting for transfers between devices  150 us (66%)
  other arithmetic  21.6 us (10%)
  starting transfers between devices  18.2 us (8%)
  between operations  17.4 us (8%)
  local copies, waits for them, and re-layouts  13.9 us (6%)
    psum x1, waiting for transfers between devices, per_device(): design_slab = lax.psum(design_slab, 'angle')  83.8 us
    reduce_scatter x1, waiting for transfers between devices, per_device(): lax.psum_scatter(even_slab, 'slab', scatter_dimension=1, tiled=True)  53.3 us
    ppermute x4, waiting for transfers between devices, from_behind(): return lax.ppermute(block, axis, route)  12.1 us
    ppermute x4, starting transfers between devices, from_behind(): return lax.ppermute(block, axis, route)  10.6 us
    unnamed x39, local copies, waits for them, and re-layouts  6.19 us
    add x2, other arithmetic, per_device(): re_part = re_part + e_field * jnp.cos(step_phase[step_index])  5.24 us
    another operation x3, other arithmetic, curl_ahead(): return jnp.stack([curl_x, curl_y, curl_z], axis=1)  4.9 us
  transfers between devices with their start and end apart: 8, of which 6 were waited for; matrix products, arithmetic and copies ran while one was open for 8% of the time, Pallas kernels for 0%

commit v1 on v0

v1 whole, which is shorter than its diff:
```python
import functools

import jax
import jax.numpy as jnp
from jax import lax
from jax.experimental import pallas as pl
from jax.experimental.pallas import tpu as pltpu
from jax.sharding import PartitionSpec as P

MESH = pl.DeviceIdType.MESH
F32 = jnp.float32
N = 128
NP = 4
PAD = 136
R = 32
TAPS = (0.375, 0.25, 0.0625)


def lane_index(rows):
    return lax.broadcasted_iota(jnp.int32, (rows, N), 1)


def next_y(v):
    return jnp.where(lane_index(v.shape[0]) < N - 1, pltpu.roll(v, N - 1, 1), 0.0)


def prev_y(v):
    return jnp.where(lane_index(v.shape[0]) > 0, pltpu.roll(v, 1, 1), 0.0)


def chunks(body):
    def step(i, carry):
        body(pl.multiple_of(i * R, R))
        return carry

    lax.fori_loop(0, N // R, step, 0)


def filter_matrix(mirror):
    row = lax.broadcasted_iota(jnp.int32, (N, N), 0)
    col = lax.broadcasted_iota(jnp.int32, (N, N), 1)

    def taps(distance):
        out = jnp.zeros((N, N), F32)
        for k, tap in enumerate(TAPS):
            out = jnp.where(jnp.abs(distance) == k, tap, out)
        return out

    out = taps(row - col)
    if mirror:
        out = out + taps(row - (N - 1 - col))
    return out


def three_parts(v):
    high = v.astype(jnp.bfloat16)
    rest = v - high.astype(F32)
    mid = rest.astype(jnp.bfloat16)
    low = (rest - mid.astype(F32)).astype(jnp.bfloat16)
    return high, mid, low


def kernel(ns, na, f, sp, ie, ph, fo, so, g, E, H, k, e0h, keep, dz, p1s, p2s, qs, p1r, p2r, qr,
           epsu, epsl, gbuf, r1, r2, in_sem, dn_s, dn_r, up_s, up_r, g1_s, g1_r, g2_s, g2_r):
    slab = lax.axis_index("slab")
    ang = lax.axis_index("angle")
    cols = N // ns
    lo_design, hi_design = ns // 2 - 1, ns // 2
    has_below, has_above = slab > 0, slab < ns - 1
    is_design = jnp.logical_or(slab == lo_design, slab == hi_design)
    below, above = (slab - 1, ang), (slab + 1, ang)
    bar = pltpu.get_barrier_semaphore()

    def signal(device):
        pl.semaphore_signal(bar, inc=1, device_id=device, device_id_type=MESH)

    pl.when(has_below)(lambda: signal(below))
    pl.when(has_above)(lambda: signal(above))
    for d in (lo_design, hi_design):
        pl.when(slab != d)(functools.partial(signal, (d, ang)))
    for j in range(1, na):
        signal((slab, lax.rem(ang + j, na)))

    loads = []
    for s in range(2):
        loads.append(pltpu.make_async_copy(f.at[0, s, 0], E.at[s, :, 0:NP, 0:N], in_sem.at[4 * s]))
        loads.append(pltpu.make_async_copy(f.at[0, s, 1], H.at[s, :, 1 : NP + 1, 8:PAD], in_sem.at[4 * s + 1]))
        loads.append(pltpu.make_async_copy(f.at[0, s, 0, 0:2, 0], keep.at[s, :, 8:PAD], in_sem.at[4 * s + 2]))
        loads.append(pltpu.make_async_copy(sp.at[0, s], so.at[0, s], in_sem.at[4 * s + 3]))
    load_eps = pltpu.make_async_copy(ie, k, in_sem.at[8])
    for i in (0, 1):
        loads[i].start()
    load_eps.start()
    for i in (2, 4, 5, 6, 3, 7):
        loads[i].start()

    for s in range(2):
        for c in range(3):
            for z in range(NP):
                E[s, c, z, N:PAD] = jnp.zeros((PAD - N, N), F32)
                H[s, c, z + 1, 0:8] = jnp.zeros((8, N), F32)
        for c in range(2):
            e0h[s, c, 0:8] = jnp.zeros((8, N), F32)
            keep[s, c, 0:8] = jnp.zeros((8, N), F32)
        dz[s, N:PAD] = jnp.zeros((PAD - N, N), F32)

    @pl.when(slab == 0)
    def _():
        p1r[...] = jnp.zeros_like(p1r)
        p2r[...] = jnp.zeros_like(p2r)
        epsl[...] = jnp.zeros_like(epsl)

    @pl.when(slab == ns - 1)
    def _():
        e0h[...] = jnp.zeros_like(e0h)
        qr[...] = jnp.zeros_like(qr)
        epsu[...] = jnp.zeros_like(epsu)

    def down(i, src, dst):
        return pltpu.make_async_remote_copy(
            src_ref=src, dst_ref=dst, send_sem=dn_s.at[i], recv_sem=dn_r.at[i], device_id=below, device_id_type=MESH)

    def up(i, src, dst):
        return pltpu.make_async_remote_copy(
            src_ref=src, dst_ref=dst, send_sem=up_s.at[i], recv_sem=up_r.at[i], device_id=above, device_id_type=MESH)

    down_eps = down(4, ie.at[0], epsu)
    up_eps = up(4, ie.at[NP - 1], epsl)
    down_e0 = [down(s, f.at[0, s, 0, 0:2, 0], e0h.at[s, :, 8:PAD]) for s in range(2)]
    down_q = [down(2 + s, qs.at[s], qr.at[s]) for s in range(2)]
    up_p1 = [up(s, p1s.at[s], p1r.at[s]) for s in range(2)]
    up_p2 = [up(2 + s, p2s.at[s], p2r.at[s]) for s in range(2)]
    downs = [down_eps] + down_e0 + down_q
    ups = [up_eps] + up_p1 + up_p2

    def h_new(s, z, r, top):
        rows, ahead = pl.ds(r, R), pl.ds(r + 1, R)
        ex, ey, ez = (E[s, c, z, rows] for c in range(3))
        if top:
            dzx, dzy = -ex, -ey
        else:
            dzx, dzy = E[s, 0, z + 1, rows] - ex, E[s, 1, z + 1, rows] - ey
        hx, hy, hz = (H[s, c, z + 1, pl.ds(r + 8, R)] for c in range(3))
        hx = hx - 0.5 * ((next_y(ez) - ez) - dzy)
        hy = hy - 0.5 * (dzx - (E[s, 2, z, ahead] - ez))
        hz = hz - 0.5 * ((E[s, 1, z, ahead] - ey) - (next_y(ex) - ex))
        return hx, hy, hz

    def e_new(s, z, r, bottom):
        rows, behind = pl.ds(r + 8, R), pl.ds(r + 7, R)
        hx, hy, hz = (H[s, c, z + 1, rows] for c in range(3))
        if bottom:
            dzx, dzy = hx, hy
        else:
            dzx, dzy = hx - H[s, 0, z, rows], hy - H[s, 1, z, rows]
        kk = 0.5 * k[z, pl.ds(r, R)]
        old = tuple(E[s, c, z, pl.ds(r, R)] for c in range(3))
        ex = old[0] + kk * ((hz - prev_y(hz)) - dzy)
        ey = old[1] + kk * (dzx - (hz - H[s, 2, z + 1, behind]))
        ez = old[2] + kk * ((hy - H[s, 1, z + 1, behind]) - (hx - prev_y(hx)))
        return old, (ex, ey, ez)

    def first_step(s):
        def h_step(r):
            for z in range(NP):
                new = h_new(s, z, r, z == NP - 1)
                for c in range(3):
                    H[s, c, z + 1, pl.ds(r + 8, R)] = new[c]
                if z == NP - 1:
                    p1s[s, 0, pl.ds(r, R)] = new[0]
                    p1s[s, 1, pl.ds(r, R)] = new[1]

        chunks(h_step)

        def e_step(r):
            for z in range(NP):
                _, new = e_new(s, z, r, z == 0)
                for c in range(3):
                    E[s, c, z, pl.ds(r, R)] = new[c]
                if z == 0:
                    qs[s, 0, pl.ds(r, R)] = new[0]
                    qs[s, 1, pl.ds(r, R)] = new[1]

        chunks(e_step)

        def h_ahead(r):
            new = h_new(s, NP - 1, r, True)
            p2s[s, 0, pl.ds(r, R)] = new[0]
            p2s[s, 1, pl.ds(r, R)] = new[1]

        chunks(h_ahead)

    edge = jnp.where(has_below, 0.5, 0.0).astype(F32)

    def corrections(s):
        def spread(r):
            rows, behind = pl.ds(r + 8, R), pl.ds(r + 7, R)
            dx, dy = edge * keep[s, 1, rows], -edge * keep[s, 0, rows]
            kl = 0.5 * epsl[pl.ds(r, R)]
            dz[s, pl.ds(r, R)] = kl * ((dy + edge * keep[s, 0, behind]) - (dx - prev_y(dx)))

        chunks(spread)

        def fix(r):
            mid, rows, behind, ahead = pl.ds(r, R), pl.ds(r + 8, R), pl.ds(r + 7, R), pl.ds(r + 1, R)
            dx, dy = 0.5 * e0h[s, 1, rows], -0.5 * e0h[s, 0, rows]
            hx, hy = H[s, 0, NP, rows] + dx, H[s, 1, NP, rows] + dy
            H[s, 0, NP, rows] = hx
            H[s, 1, NP, rows] = hy
            k3 = 0.5 * k[NP - 1, mid]
            E[s, 0, NP - 1, mid] = E[s, 0, NP - 1, mid] - k3 * dy
            E[s, 1, NP - 1, mid] = E[s, 1, NP - 1, mid] + k3 * dx
            E[s, 2, NP - 1, mid] = E[s, 2, NP - 1, mid] + k3 * (
                (dy + 0.5 * e0h[s, 0, behind]) - (dx - prev_y(dx)))
            ku = 0.5 * epsu[mid]
            E[s, 0, NP, mid] = qr[s, 0, mid] + ku * hy
            E[s, 1, NP, mid] = qr[s, 1, mid] - ku * hx
            dx, dy = edge * keep[s, 1, rows], -edge * keep[s, 0, rows]
            k0, kl = 0.5 * k[0, mid], 0.5 * epsl[mid]
            ex = E[s, 0, 0, mid] + k0 * (p1r[s, 1, mid] + dy)
            ey = E[s, 1, 0, mid] - k0 * (p1r[s, 0, mid] + dx)
            E[s, 0, 0, mid] = ex
            E[s, 1, 0, mid] = ey
            d = dz[s, mid]
            H[s, 0, 0, rows] = p2r[s, 0, mid] + dx - 0.5 * (next_y(d) - d) + (edge * ey - 0.5 * kl * dx)
            H[s, 1, 0, rows] = p2r[s, 1, mid] + dy + 0.5 * (dz[s, ahead] - d) - (edge * ex + 0.5 * kl * dy)

        chunks(fix)

    def second_step(s):
        def h_step(r):
            for z in range(NP):
                new = h_new(s, z, r, False)
                for c in range(3):
                    H[s, c, z + 1, pl.ds(r + 8, R)] = new[c]
                    fo[0, s, 1, c, z, pl.ds(r, R)] = new[c]

        chunks(h_step)

        c0, s0, c1, s1 = (op(jnp.full((1, N), ph[t], F32)) for t in range(2) for op in (jnp.cos, jnp.sin))

        def e_step(r):
            for z in range(NP):
                old, new = e_new(s, z, r, False)
                for c in range(3):
                    rows = pl.ds(r, R)
                    fo[0, s, 0, c, z, rows] = new[c]
                    so[0, s, 0, c, z, rows] = so[0, s, 0, c, z, rows] + old[c] * c0 + new[c] * c1
                    so[0, s, 1, c, z, rows] = so[0, s, 1, c, z, rows] + old[c] * s0 + new[c] * s1

        chunks(e_step)

    loads[0].wait()
    loads[1].wait()
    load_eps.wait()
    first_step(0)
    incoming = (na - 1) + jnp.where(has_below, 1, 0) + jnp.where(has_above, 1, 0) + jnp.where(is_design, ns - 1, 0)
    pl.semaphore_wait(bar, incoming)

    @pl.when(has_below)
    def _():
        down_eps.start()
        down_e0[0].start()
        down_q[0].start()
        down_e0[1].start()

    @pl.when(has_above)
    def _():
        up_eps.start()
        up_p1[0].start()
        up_p2[0].start()

    loads[4].wait()
    loads[5].wait()
    first_step(1)
    pl.when(has_below)(lambda: down_q[1].start())

    @pl.when(has_above)
    def _():
        up_p1[1].start()
        up_p2[1].start()

    for i in (2, 6, 3, 7):
        loads[i].wait()

    for s in range(2):
        @pl.when(has_above)
        def _():
            if s == 0:
                down_eps.wait_recv()
            down_e0[s].wait_recv()
            down_q[s].wait_recv()

        @pl.when(has_below)
        def _():
            if s == 0:
                up_eps.wait_recv()
            up_p1[s].wait_recv()
            up_p2[s].wait_recv()

        corrections(s)
        second_step(s)

    def to_owner(side, owner):
        return pltpu.make_async_remote_copy(
            src_ref=gbuf.at[:, pl.ds(owner * cols, cols)], dst_ref=r1.at[pl.ds(side * NP, NP)],
            send_sem=g1_s.at[owner], recv_sem=g1_r.at[side], device_id=(owner, ang), device_id_type=MESH)

    @pl.when(is_design)
    def _():
        fy = filter_matrix(False).astype(jnp.bfloat16)
        mx = (filter_matrix(True) * (0.5 / na)).astype(jnp.bfloat16)

        def plane(z, carry):
            total = jnp.zeros((N, N), F32)
            for c in range(3):
                total = total + so[0, 0, 0, c, z] * so[0, 1, 0, c, z] - so[0, 0, 1, c, z] * so[0, 1, 1, c, z]
            along_y = sum(jnp.dot(p, fy, preferred_element_type=F32) for p in three_parts(total))
            gbuf[z] = sum(jnp.dot(mx, p, preferred_element_type=F32) for p in three_parts(along_y))
            return carry

        lax.fori_loop(0, NP, plane, 0)

    for side, d in enumerate((lo_design, hi_design)):
        @pl.when(slab == d)
        def _():
            for owner in range(ns):
                if owner != d:
                    to_owner(side, owner).start()
            r1[side * NP : (side + 1) * NP] = gbuf[:, d * cols : (d + 1) * cols]

    for side, d in enumerate((lo_design, hi_design)):
        pl.when(slab != d)(lambda: to_owner(side, slab).wait_recv())

    def to_peer(j):
        return pltpu.make_async_remote_copy(
            src_ref=r1, dst_ref=r2.at[ang], send_sem=g2_s.at[j], recv_sem=g2_r.at[ang],
            device_id=(slab, lax.rem(ang + j, na)), device_id_type=MESH)

    def from_peer(j):
        other = lax.rem(ang + j, na)
        return pltpu.make_async_remote_copy(
            src_ref=r1, dst_ref=r2.at[other], send_sem=g2_s.at[j], recv_sem=g2_r.at[other],
            device_id=(slab, other), device_id_type=MESH)

    for j in range(1, na):
        to_peer(j).start()
    r2[ang] = r1[...]
    for j in range(1, na):
        from_peer(j).wait_recv()
    total = r2[0]
    for j in range(1, na):
        total = total + r2[j]
    g[...] = total

    for j in range(1, na):
        to_peer(j).wait_send()

    @pl.when(has_below)
    def _():
        for c in downs:
            c.wait_send()

    @pl.when(has_above)
    def _():
        for c in ups:
            c.wait_send()

    for side, d in enumerate((lo_design, hi_design)):
        @pl.when(slab == d)
        def _():
            for owner in range(ns):
                if owner != d:
                    to_owner(side, owner).wait_send()


def write_out(a, b, c, x, y, z, sem):
    copies = [pltpu.make_async_copy(p, q, sem.at[i]) for i, (p, q) in enumerate(((a, x), (b, y), (c, z)))]
    for copy in copies:
        copy.start()
    for copy in copies:
        copy.wait()


def per_device(fields, spectra, inv_eps, step_phase):
    ns, na = lax.axis_size("slab"), lax.axis_size("angle")
    cols = N // ns
    shape = fields.shape
    grad = (2 * NP, cols, N)
    vmem = pl.BlockSpec(memory_space=pltpu.VMEM)
    hbm = pl.BlockSpec(memory_space=pltpu.HBM)
    outs = (shape, shape, grad)
    dma = pltpu.SemaphoreType.DMA
    planes = pltpu.VMEM((2, 2, N, N), F32)
    results = pl.pallas_call(
        functools.partial(kernel, ns, na),
        out_shape=[pltpu.VMEM(s, F32) for s in outs],
        in_specs=[hbm, hbm, hbm, pl.BlockSpec(memory_space=pltpu.SMEM)],
        out_specs=[vmem] * 3,
        scratch_shapes=[
            pltpu.VMEM((2, 3, NP + 1, PAD, N), F32),
            pltpu.VMEM((2, 3, NP + 1, PAD, N), F32),
            pltpu.VMEM((NP, N, N), F32),
            pltpu.VMEM((2, 2, PAD, N), F32),
            pltpu.VMEM((2, 2, PAD, N), F32),
            pltpu.VMEM((2, PAD, N), F32),
            planes, planes, planes, planes, planes, planes,
            pltpu.VMEM((N, N), F32),
            pltpu.VMEM((N, N), F32),
            pltpu.VMEM((NP, N, N), F32),
            pltpu.VMEM(grad, F32),
            pltpu.VMEM((na,) + grad, F32),
            dma((9,)), dma((5,)), dma((5,)), dma((5,)), dma((5,)),
            dma((ns,)), dma((2,)), dma((na,)), dma((na,)),
        ],
        compiler_params=pltpu.CompilerParams(
            collective_id=0, has_side_effects=True, vmem_limit_bytes=48 * 2**20),
        name="steps",
    )(fields, spectra, inv_eps, step_phase)
    return tuple(pl.pallas_call(
        write_out,
        out_shape=[jax.ShapeDtypeStruct(s, F32) for s in outs],
        in_specs=[vmem] * 3,
        out_specs=[pl.BlockSpec(memory_space=pl.ANY)] * 3,
        scratch_shapes=[dma((3,))],
        compiler_params=pltpu.CompilerParams(has_side_effects=True, vmem_limit_bytes=2**20),
        name="write_out",
    )(*(pltpu.with_memory_space_constraint(r, pltpu.VMEM) for r in results)))


def solution(mesh):
    cells = P("angle", None, None, None, "slab", None, None)
    return jax.shard_map(
        per_device,
        mesh=mesh,
        in_specs=(cells, cells, P("slab", None, None), P()),
        out_specs=(cells, cells, P(None, "slab", None)),
        check_vma=False,
    )
```

time: 227 us -> 34.1 us (0.15)
  the two profiles are of different devices: /device:TPU:1 before, /device:TPU:24 now
where the time goes in v1:
time: 34.1 us; the launch traced here: 34 us
  Pallas kernels  33.3 us (98%)
  between operations  0.64 us (2%)
    pallas_call x1, Pallas kernels, per_device(): pl.pallas_call(functools.partial(kernel, ns, na), out_shape=[pltpu.VMEM(s...  30.6 us
    pallas_call x1, Pallas kernels, per_device(): pl.pallas_call(write_out, out_shape=[jax.ShapeDtypeStruct(s, F32) for s i...  2.73 us

profile of v1, /device:TPU:24, one launch (start us, length us, event | category | flops | bytes accessed | tf_op | source)
XLA Modules:
  0.0 34.0 jit_solution(2696221970008898004)
XLA Ops:
  0.6 30.6 %steps.1 = (f32[1,2,2,3,4,128,128]{6,5,4,3,2,1,0:T(8,128)S(1)}, f32[1,2,2,3,4,128,128]{6,5,4,3,2,1,0:T(8,128)S(1)}, f32[8,8,128]{2,1,0:T(8,128)S(1)}) custom-call(f32[1,2,2,3,4,128,128]{6,5,4,3,2,1,0:T(8,128)} %f.1, f32[1,2,2,3,4,128,128]{6,5,4,3,2,1,0:T(8,128)} %sp.1, f32[4,128,128]{2,1,0:T(8,128)} %ie.1, f32[2]{0:T(128)} %ph.1), custom_call_target="tpu_custom_call" | custom-call | tf_op jit(solution)/shard_map/steps/pallas_call | solution.py:395
  31.3 2.7 %write_out.1 = (f32[1,2,2,3,4,128,128]{6,5,4,3,2,1,0:T(8,128)}, f32[1,2,2,3,4,128,128]{6,5,4,3,2,1,0:T(8,128)}, f32[8,8,128]{2,1,0:T(8,128)}) custom-call(f32[1,2,2,3,4,128,128]{6,5,4,3,2,1,0:T(8,128)S(1)} %get-tuple-element.6.a, f32[1,2,2,3,4,128,128]{6,5,4,3,2,1,0:T(8,128)S(1)} %get-tuple-element.7.b, f32[8,8,128]{2,1,0:T(8,128)S(1)} %get-tuple-element.8.c), custom_call_target="tpu_custom_call" | custom-call | tf_op jit(solution)/shard_map/write_out/pallas_call | solution.py:420

commit v2 on v1

--- a/solution.py
+++ b/solution.py
@@ -61,7 +61,7 @@
 
 
 def kernel(ns, na, f, sp, ie, ph, fo, so, g, E, H, k, e0h, keep, dz, p1s, p2s, qs, p1r, p2r, qr,
-           epsu, epsl, gbuf, r1, r2, in_sem, dn_s, dn_r, up_s, up_r, g1_s, g1_r, g2_s, g2_r):
+           epsu, epsl, dens, fy, mx, gbuf, r1, r2, rb, in_sem, dn_s, dn_r, up_s, up_r, g1_s, g1_r, g2_s, g2_r, rl_s, rl_r):
     slab = lax.axis_index("slab")
     ang = lax.axis_index("angle")
     cols = N // ns
@@ -69,6 +69,7 @@
     has_below, has_above = slab > 0, slab < ns - 1
     is_design = jnp.logical_or(slab == lo_design, slab == hi_design)
     below, above = (slab - 1, ang), (slab + 1, ang)
+    relay_up, relay_down = 1, ns - 1
     bar = pltpu.get_barrier_semaphore()
 
     def signal(device):
@@ -78,6 +79,8 @@
     pl.when(has_above)(lambda: signal(above))
     for d in (lo_design, hi_design):
         pl.when(slab != d)(functools.partial(signal, (d, ang)))
+    pl.when(slab == hi_design)(lambda: signal((relay_up, ang)))
+    pl.when(slab == lo_design)(lambda: signal((relay_down, ang)))
     for j in range(1, na):
         signal((slab, lax.rem(ang + j, na)))
 
@@ -130,8 +133,40 @@
     down_q = [down(2 + s, qs.at[s], qr.at[s]) for s in range(2)]
     up_p1 = [up(s, p1s.at[s], p1r.at[s]) for s in range(2)]
     up_p2 = [up(2 + s, p2s.at[s], p2r.at[s]) for s in range(2)]
-    downs = [down_eps] + down_e0 + down_q
-    ups = [up_eps] + up_p1 + up_p2
+    def relayed(s, c, src, device):
+        return pltpu.make_async_remote_copy(
+            src_ref=src.at[s, c], dst_ref=rb.at[s, c], send_sem=rl_s.at[2 * s + c], recv_sem=rl_r.at[2 * s + c],
+            device_id=(device, ang), device_id_type=MESH)
+
+    def passed_on(s, c, dst, sems, device):
+        return pltpu.make_async_remote_copy(
+            src_ref=rb.at[s, c], dst_ref=dst.at[s, c], send_sem=rl_s.at[2 * s + c], recv_sem=sems.at[2 + s],
+            device_id=(device, ang), device_id_type=MESH)
+
+    def send_q(s):
+        pl.when(jnp.logical_and(has_below, slab != hi_design))(lambda: down_q[s].start())
+
+        @pl.when(slab == hi_design)
+        def _():
+            for c in range(2):
+                relayed(s, c, qs, relay_down).start()
+
+    def send_p2(s):
+        pl.when(jnp.logical_and(has_above, slab != lo_design))(lambda: up_p2[s].start())
+
+        @pl.when(slab == lo_design)
+        def _():
+            for c in range(2):
+                relayed(s, c, p2s, relay_up).start()
+
+    def pass_on(s):
+        for relay, src, dst, sems, device in (
+            (relay_up, p2s, p2r, up_r, hi_design), (relay_down, qs, qr, dn_r, lo_design)):
+            @pl.when(slab == relay)
+            def _():
+                for c in range(2):
+                    relayed(s, c, src, relay).wait_recv()
+                    passed_on(s, c, dst, sems, device).start()
 
     def h_new(s, z, r, top):
         rows, ahead = pl.ds(r, R), pl.ds(r + 1, R)
@@ -192,17 +227,9 @@
 
     edge = jnp.where(has_below, 0.5, 0.0).astype(F32)
 
-    def corrections(s):
-        def spread(r):
-            rows, behind = pl.ds(r + 8, R), pl.ds(r + 7, R)
-            dx, dy = edge * keep[s, 1, rows], -edge * keep[s, 0, rows]
-            kl = 0.5 * epsl[pl.ds(r, R)]
-            dz[s, pl.ds(r, R)] = kl * ((dy + edge * keep[s, 0, behind]) - (dx - prev_y(dx)))
-
-        chunks(spread)
-
+    def fix_above(s):
         def fix(r):
-            mid, rows, behind, ahead = pl.ds(r, R), pl.ds(r + 8, R), pl.ds(r + 7, R), pl.ds(r + 1, R)
+            mid, rows, behind = pl.ds(r, R), pl.ds(r + 8, R), pl.ds(r + 7, R)
             dx, dy = 0.5 * e0h[s, 1, rows], -0.5 * e0h[s, 0, rows]
             hx, hy = H[s, 0, NP, rows] + dx, H[s, 1, NP, rows] + dy
             H[s, 0, NP, rows] = hx
@@ -215,6 +242,20 @@
             ku = 0.5 * epsu[mid]
             E[s, 0, NP, mid] = qr[s, 0, mid] + ku * hy
             E[s, 1, NP, mid] = qr[s, 1, mid] - ku * hx
+
+        chunks(fix)
+
+    def fix_below(s):
+        def spread(r):
+            rows, behind = pl.ds(r + 8, R), pl.ds(r + 7, R)
+            dx, dy = edge * keep[s, 1, rows], -edge * keep[s, 0, rows]
+            kl = 0.5 * epsl[pl.ds(r, R)]
+            dz[s, pl.ds(r, R)] = kl * ((dy + edge * keep[s, 0, behind]) - (dx - prev_y(dx)))
+
+        chunks(spread)
+
+        def fix(r):
+            mid, rows, ahead = pl.ds(r, R), pl.ds(r + 8, R), pl.ds(r + 1, R)
             dx, dy = edge * keep[s, 1, rows], -edge * keep[s, 0, rows]
             k0, kl = 0.5 * k[0, mid], 0.5 * epsl[mid]
             ex = E[s, 0, 0, mid] + k0 * (p1r[s, 1, mid] + dy)
@@ -227,9 +268,9 @@
 
         chunks(fix)
 
-    def second_step(s):
+    def second_h(s, planes):
         def h_step(r):
-            for z in range(NP):
+            for z in planes:
                 new = h_new(s, z, r, False)
                 for c in range(3):
                     H[s, c, z + 1, pl.ds(r + 8, R)] = new[c]
@@ -237,141 +278,185 @@
 
         chunks(h_step)
 
+    def second_e(s, planes):
         c0, s0, c1, s1 = (op(jnp.full((1, N), ph[t], F32)) for t in range(2) for op in (jnp.cos, jnp.sin))
 
         def e_step(r):
-            for z in range(NP):
+            for z in planes:
                 old, new = e_new(s, z, r, False)
+                total = jnp.zeros((R, N), F32)
                 for c in range(3):
                     rows = pl.ds(r, R)
                     fo[0, s, 0, c, z, rows] = new[c]
-                    so[0, s, 0, c, z, rows] = so[0, s, 0, c, z, rows] + old[c] * c0 + new[c] * c1
-                    so[0, s, 1, c, z, rows] = so[0, s, 1, c, z, rows] + old[c] * s0 + new[c] * s1
+                    re = so[0, s, 0, c, z, rows] + old[c] * c0 + new[c] * c1
+                    im = so[0, s, 1, c, z, rows] + old[c] * s0 + new[c] * s1
+                    so[0, s, 0, c, z, rows] = re
+                    so[0, s, 1, c, z, rows] = im
+                    if s == 1:
+                        total = total + so[0, 0, 0, c, z, rows] * re - so[0, 0, 1, c, z, rows] * im
+                if s == 1:
+                    dens[z, rows] = total
 
         chunks(e_step)
+
+    def lower_planes(s):
+        @pl.when(has_below)
+        def _():
+            if s == 0:
+                up_eps.wait_recv()
+            up_p1[s].wait_recv()
+            up_p2[s].wait_recv()
+
+        fix_below(s)
+        second_h(s, (0,))
+        second_e(s, (0, 1))
+
+    def upper_planes(s):
+        @pl.when(has_above)
+        def _():
+            if s == 0:
+                down_eps.wait_recv()
+            down_e0[s].wait_recv()
+            down_q[s].wait_recv()
+
+        fix_above(s)
+        second_h(s, (2, 3))
+        second_e(s, (2, 3))
 
     loads[0].wait()
     loads[1].wait()
     load_eps.wait()
     first_step(0)
     incoming = (na - 1) + jnp.where(has_below, 1, 0) + jnp.where(has_above, 1, 0) + jnp.where(is_design, ns - 1, 0)
+    incoming = incoming + jnp.where(jnp.logical_or(slab == relay_up, slab == relay_down), 1, 0)
     pl.semaphore_wait(bar, incoming)
 
     @pl.when(has_below)
     def _():
         down_eps.start()
         down_e0[0].start()
-        down_q[0].start()
         down_e0[1].start()
 
     @pl.when(has_above)
     def _():
         up_eps.start()
         up_p1[0].start()
-        up_p2[0].start()
-
+
+    send_q(0)
+    send_p2(0)
     loads[4].wait()
     loads[5].wait()
     first_step(1)
-    pl.when(has_below)(lambda: down_q[1].start())
-
-    @pl.when(has_above)
-    def _():
-        up_p1[1].start()
-        up_p2[1].start()
-
+    pl.when(has_above)(lambda: up_p1[1].start())
+    send_q(1)
+    send_p2(1)
+    for s in range(2):
+        pass_on(s)
+    for s in range(2):
+        second_h(s, (1,))
+    fy[...] = filter_matrix(False).astype(jnp.bfloat16)
+    mx[...] = (filter_matrix(True) * (0.5 / na)).astype(jnp.bfloat16)
     for i in (2, 6, 3, 7):
         loads[i].wait()
 
-    for s in range(2):
-        @pl.when(has_above)
-        def _():
-            if s == 0:
-                down_eps.wait_recv()
-            down_e0[s].wait_recv()
-            down_q[s].wait_recv()
-
-        @pl.when(has_below)
-        def _():
-            if s == 0:
-                up_eps.wait_recv()
-            up_p1[s].wait_recv()
-            up_p2[s].wait_recv()
-
-        corrections(s)
-        second_step(s)
-
-    def to_owner(side, owner):
-        return pltpu.make_async_remote_copy(
-            src_ref=gbuf.at[:, pl.ds(owner * cols, cols)], dst_ref=r1.at[pl.ds(side * NP, NP)],
-            send_sem=g1_s.at[owner], recv_sem=g1_r.at[side], device_id=(owner, ang), device_id_type=MESH)
-
-    @pl.when(is_design)
-    def _():
-        fy = filter_matrix(False).astype(jnp.bfloat16)
-        mx = (filter_matrix(True) * (0.5 / na)).astype(jnp.bfloat16)
-
-        def plane(z, carry):
-            total = jnp.zeros((N, N), F32)
-            for c in range(3):
-                total = total + so[0, 0, 0, c, z] * so[0, 1, 0, c, z] - so[0, 0, 1, c, z] * so[0, 1, 1, c, z]
-            along_y = sum(jnp.dot(p, fy, preferred_element_type=F32) for p in three_parts(total))
-            gbuf[z] = sum(jnp.dot(mx, p, preferred_element_type=F32) for p in three_parts(along_y))
-            return carry
-
-        lax.fori_loop(0, NP, plane, 0)
+    half = NP // 2
+
+    def to_owner(part, side, owner):
+        return pltpu.make_async_remote_copy(
+            src_ref=gbuf.at[part, :, pl.ds(owner * cols, cols)], dst_ref=r1.at[part, pl.ds(side * half, half)],
+            send_sem=g1_s.at[part, owner], recv_sem=g1_r.at[part, side], device_id=(owner, ang), device_id_type=MESH)
+
+    def spread_density(part, first, side):
+        planes = dens[first : first + half].reshape(half * N, N)
+        along_y = sum(jnp.dot(p, fy[...], preferred_element_type=F32) for p in three_parts(planes))
+        beside = jnp.concatenate([along_y[z * N : (z + 1) * N] for z in range(half)], axis=1)
+        both = sum(jnp.dot(mx[...], p, preferred_element_type=F32) for p in three_parts(beside))
+        for z in range(half):
+            gbuf[part, z] = both[:, z * N : (z + 1) * N]
+        d = (lo_design, hi_design)[side]
+        for owner in range(ns):
+            if owner != d:
+                to_owner(part, side, owner).start()
+        r1[part, side * half : (side + 1) * half] = gbuf[part, :, d * cols : (d + 1) * cols]
+
+    second = (lower_planes, upper_planes)
+    for odd in (0, 1):
+        @pl.when(slab % 2 == odd)
+        def _():
+            design = (hi_design, lo_design)[odd]
+            for part in (0, 1):
+                upper = part if odd else 1 - part
+                for s in range(2):
+                    second[upper](s)
+                pl.when(slab == design)(functools.partial(spread_density, part, half * upper, 1 - odd))
+
+    def to_peer(part, j):
+        return pltpu.make_async_remote_copy(
+            src_ref=r1.at[part], dst_ref=r2.at[part, ang], send_sem=g2_s.at[part, j], recv_sem=g2_r.at[part, ang],
+            device_id=(slab, lax.rem(ang + j, na)), device_id_type=MESH)
+
+    def from_peer(part, j):
+        other = lax.rem(ang + j, na)
+        return pltpu.make_async_remote_copy(
+            src_ref=r1.at[part], dst_ref=r2.at[part, other], send_sem=g2_s.at[part, j],
+            recv_sem=g2_r.at[part, other], device_id=(slab, other), device_id_type=MESH)
+
+    for part in (0, 1):
+        for side, d in enumerate((lo_design, hi_design)):
+            pl.when(slab != d)(lambda: to_owner(part, side, slab).wait_recv())
+        for j in range(1, na):
+            to_peer(part, j).start()
+        r2[part, ang] = r1[part]
+    for part in (0, 1):
+        for j in range(1, na):
+            from_peer(part, j).wait_recv()
+        total = r2[part, 0]
+        for j in range(1, na):
+            total = total + r2[part, j]
+        if part == 0:
+            g[0:half] = total[0:half]
+            g[NP + half :] = total[half:]
+        else:
+            g[half : NP + half] = total
+
+    for part in (0, 1):
+        for j in range(1, na):
+            to_peer(part, j).wait_send()
+
+    @pl.when(has_below)
+    def _():
+        for c in [down_eps] + down_e0:
+            c.wait_send()
+
+    @pl.when(has_above)
+    def _():
+        for c in [up_eps] + up_p1:
+            c.wait_send()
+
+    @pl.when(jnp.logical_and(has_below, slab != hi_design))
+    def _():
+        for c in down_q:
+            c.wait_send()
+
+    @pl.when(jnp.logical_and(has_above, slab != lo_design))
+    def _():
+        for c in up_p2:
+            c.wait_send()
+
+    for d, src in ((hi_design, qs), (lo_design, p2s), (relay_up, rb), (relay_down, rb)):
+        @pl.when(slab == d)
+        def _():
+            for s in range(2):
+                for c in range(2):
+                    relayed(s, c, src, d).wait_send()
 
     for side, d in enumerate((lo_design, hi_design)):
         @pl.when(slab == d)
         def _():
             for owner in range(ns):
                 if owner != d:
-                    to_owner(side, owner).start()
-            r1[side * NP : (side + 1) * NP] = gbuf[:, d * cols : (d + 1) * cols]
-
-    for side, d in enumerate((lo_design, hi_design)):
-        pl.when(slab != d)(lambda: to_owner(side, slab).wait_recv())
-
-    def to_peer(j):
-        return pltpu.make_async_remote_copy(
-            src_ref=r1, dst_ref=r2.at[ang], send_sem=g2_s.at[j], recv_sem=g2_r.at[ang],
-            device_id=(slab, lax.rem(ang + j, na)), device_id_type=MESH)
-
-    def from_peer(j):
-        other = lax.rem(ang + j, na)
-        return pltpu.make_async_remote_copy(
-            src_ref=r1, dst_ref=r2.at[other], send_sem=g2_s.at[j], recv_sem=g2_r.at[other],
-            device_id=(slab, other), device_id_type=MESH)
-
-    for j in range(1, na):
-        to_peer(j).start()
-    r2[ang] = r1[...]
-    for j in range(1, na):
-        from_peer(j).wait_recv()
-    total = r2[0]
-    for j in range(1, na):
-        total = total + r2[j]
-    g[...] = total
-
-    for j in range(1, na):
-        to_peer(j).wait_send()
-
-    @pl.when(has_below)
-    def _():
-        for c in downs:
-            c.wait_send()
-
-    @pl.when(has_above)
-    def _():
-        for c in ups:
-            c.wait_send()
-
-    for side, d in enumerate((lo_design, hi_design)):
-        @pl.when(slab == d)
-        def _():
-            for owner in range(ns):
-                if owner != d:
-                    to_owner(side, owner).wait_send()
+                    for part in (0, 1):
+                        to_owner(part, side, owner).wait_send()
 
 
 def write_out(a, b, c, x, y, z, sem):
@@ -408,10 +493,14 @@
             pltpu.VMEM((N, N), F32),
             pltpu.VMEM((N, N), F32),
             pltpu.VMEM((NP, N, N), F32),
-            pltpu.VMEM(grad, F32),
-            pltpu.VMEM((na,) + grad, F32),
+            pltpu.VMEM((N, N), jnp.bfloat16),
+            pltpu.VMEM((N, N), jnp.bfloat16),
+            pltpu.VMEM((2, NP // 2, N, N), F32),
+            pltpu.VMEM((2, NP, cols, N), F32),
+            pltpu.VMEM((2, na, NP, cols, N), F32),
+            planes,
             dma((9,)), dma((5,)), dma((5,)), dma((5,)), dma((5,)),
-            dma((ns,)), dma((2,)), dma((na,)), dma((na,)),
+            dma((2, ns)), dma((2, 2)), dma((2, na)), dma((2, na)), dma((4,)), dma((4,)),
         ],
         compiler_params=pltpu.CompilerParams(
             collective_id=0, has_side_effects=True, vmem_limit_bytes=48 * 2**20),

time: 34.1 us -> 30.3 us (0.89)
  the two profiles are of different devices: /device:TPU:24 before, /device:TPU:1 now
where the time goes in v2:
time: 30.3 us; the launch traced here: 30.2 us
  Pallas kernels  29.6 us (98%)
  between operations  0.64 us (2%)
    pallas_call x1, Pallas kernels, per_device(): pl.pallas_call(functools.partial(kernel, ns, na), out_shape=[pltpu.VMEM(s...  26.8 us
    pallas_call x1, Pallas kernels, per_device(): pl.pallas_call(write_out, out_shape=[jax.ShapeDtypeStruct(s, F32) for s i...  2.73 us

profile of v2, /device:TPU:1, one launch (start us, length us, event | category | flops | bytes accessed | tf_op | source)
XLA Modules:
  0.0 30.2 jit_solution(13388372710561242732)
XLA Ops:
  0.6 26.8 %steps.1 = (f32[1,2,2,3,4,128,128]{6,5,4,3,2,1,0:T(8,128)S(1)}, f32[1,2,2,3,4,128,128]{6,5,4,3,2,1,0:T(8,128)S(1)}, f32[8,8,128]{2,1,0:T(8,128)S(1)}) custom-call(f32[1,2,2,3,4,128,128]{6,5,4,3,2,1,0:T(8,128)} %f.1, f32[1,2,2,3,4,128,128]{6,5,4,3,2,1,0:T(8,128)} %sp.1, f32[4,128,128]{2,1,0:T(8,128)} %ie.1, f32[2]{0:T(128)} %ph.1), custom_call_target="tpu_custom_call" | custom-call | tf_op jit(solution)/shard_map/steps/pallas_call | solution.py:480
  27.5 2.7 %write_out.1 = (f32[1,2,2,3,4,128,128]{6,5,4,3,2,1,0:T(8,128)}, f32[1,2,2,3,4,128,128]{6,5,4,3,2,1,0:T(8,128)}, f32[8,8,128]{2,1,0:T(8,128)}) custom-call(f32[1,2,2,3,4,128,128]{6,5,4,3,2,1,0:T(8,128)S(1)} %get-tuple-element.6.a, f32[1,2,2,3,4,128,128]{6,5,4,3,2,1,0:T(8,128)S(1)} %get-tuple-element.7.b, f32[8,8,128]{2,1,0:T(8,128)S(1)} %get-tuple-element.8.c), custom_call_target="tpu_custom_call" | custom-call | tf_op jit(solution)/shard_map/write_out/pallas_call | solution.py:509

commit v3 on v2

v3 whole, which is shorter than its diff:
```python
import functools

import jax
import jax.numpy as jnp
from jax import lax
from jax.experimental import pallas as pl
from jax.experimental.pallas import tpu as pltpu
from jax.sharding import PartitionSpec as P

MESH = pl.DeviceIdType.MESH
F32 = jnp.float32
N = 128
NP = 4
HALF = NP // 2
PAD = 136
TAPS = (0.375, 0.25, 0.0625)
E_ROWS, E_AHEAD = pl.ds(0, N), pl.ds(1, N)
H_ROWS, H_BEHIND = pl.ds(8, N), pl.ds(7, N)


def lane_index(rows):
    return lax.broadcasted_iota(jnp.int32, (rows, N), 1)


def next_y(v):
    return jnp.where(lane_index(v.shape[0]) < N - 1, pltpu.roll(v, N - 1, 1), 0.0)


def prev_y(v):
    return jnp.where(lane_index(v.shape[0]) > 0, pltpu.roll(v, 1, 1), 0.0)


def filter_matrix(mirror):
    row = lax.broadcasted_iota(jnp.int32, (N, N), 0)
    col = lax.broadcasted_iota(jnp.int32, (N, N), 1)

    def taps(distance):
        out = jnp.zeros((N, N), F32)
        for k, tap in enumerate(TAPS):
            out = jnp.where(jnp.abs(distance) == k, tap, out)
        return out

    out = taps(row - col)
    if mirror:
        out = out + taps(row - (N - 1 - col))
    return out


def three_parts(v):
    high = v.astype(jnp.bfloat16)
    rest = v - high.astype(F32)
    mid = rest.astype(jnp.bfloat16)
    low = (rest - mid.astype(F32)).astype(jnp.bfloat16)
    return high, mid, low


def kernel(ns, na, f, sp, ie, ph, fo, so, g, E, H, k, e0h, keep, dz, p1s, p2s, qs, p1r, p2r, qr,
           epsu, epsl, dens, fy, mx, gbuf, r1, r2, rb, in_sem, dn_s, dn_r, up_s, up_r, rl_s, rl_r,
           g1_s, g1_r, g2_s, g2_r):
    slab = lax.axis_index("slab")
    ang = lax.axis_index("angle")
    cols = N // ns
    lo_design, hi_design = ns // 2 - 1, ns // 2
    has_below, has_above = slab > 0, slab < ns - 1
    is_design = jnp.logical_or(slab == lo_design, slab == hi_design)
    relay_up, relay_down = 1, ns - 1
    bar = pltpu.get_barrier_semaphore()

    def signal(slab_index, angle_index):
        pl.semaphore_signal(bar, inc=1, device_id=(slab_index, angle_index), device_id_type=MESH)

    def send(src, dst, send_sem, recv_sem, slab_index, angle_index):
        return pltpu.make_async_remote_copy(
            src_ref=src, dst_ref=dst, send_sem=send_sem, recv_sem=recv_sem,
            device_id=(slab_index, angle_index), device_id_type=MESH)

    def wait_bytes(ref, sem):
        pltpu.make_async_copy(ref, ref, sem).wait()

    pl.when(has_below)(lambda: signal(slab - 1, ang))
    pl.when(has_above)(lambda: signal(slab + 1, ang))
    for d in (lo_design, hi_design):
        pl.when(slab != d)(functools.partial(signal, d, ang))
    pl.when(slab == hi_design)(lambda: signal(relay_up, ang))
    pl.when(slab == lo_design)(lambda: signal(relay_down, ang))
    for j in range(1, na):
        signal(slab, lax.rem(ang + j, na))

    for s in range(2):
        pltpu.make_async_copy(f.at[0, s, 0], E.at[s, :, 0:NP, E_ROWS], in_sem.at[s]).start()
        pltpu.make_async_copy(f.at[0, s, 1], H.at[s, :, 1 : NP + 1, H_ROWS], in_sem.at[s]).start()
        if s == 0:
            load_eps = pltpu.make_async_copy(ie, k, in_sem.at[2])
            load_eps.start()
    load_keep = pltpu.make_async_copy(f.at[0, :, 0, 0:2, 0], keep.at[:, :, H_ROWS], in_sem.at[3])
    load_keep.start()
    load_spectra = pltpu.make_async_copy(sp, so, in_sem.at[4])
    load_spectra.start()

    for s in range(2):
        for c in range(3):
            for z in range(NP):
                E[s, c, z, N:PAD] = jnp.zeros((PAD - N, N), F32)
                H[s, c, z + 1, 0:8] = jnp.zeros((8, N), F32)
        for c in range(2):
            e0h[s, c, 0:8] = jnp.zeros((8, N), F32)
            keep[s, c, 0:8] = jnp.zeros((8, N), F32)
    dz[N:PAD] = jnp.zeros((PAD - N, N), F32)

    @pl.when(slab == 0)
    def _():
        p1r[...] = jnp.zeros_like(p1r)
        p2r[...] = jnp.zeros_like(p2r)
        epsl[...] = jnp.zeros_like(epsl)

    @pl.when(slab == ns - 1)
    def _():
        e0h[...] = jnp.zeros_like(e0h)
        qr[...] = jnp.zeros_like(qr)
        epsu[...] = jnp.zeros_like(epsu)

    def down(src, dst, i):
        return send(src, dst, dn_s, dn_r.at[i], slab - 1, ang)

    def up(src, dst, i):
        return send(src, dst, up_s, up_r.at[i], slab + 1, ang)

    def send_q(s):
        pl.when(jnp.logical_and(has_below, slab != hi_design))(lambda: down(qs.at[s], qr.at[s], s).start())

        @pl.when(slab == hi_design)
        def _():
            for c in range(2):
                send(qs.at[s, c], rb.at[s, c], dn_s, rl_r.at[2 * s + c], relay_down, ang).start()

    def send_p2(s):
        pl.when(jnp.logical_and(has_above, slab != lo_design))(lambda: up(p2s.at[s], p2r.at[s], s).start())

        @pl.when(slab == lo_design)
        def _():
            for c in range(2):
                send(p2s.at[s, c], rb.at[s, c], up_s, rl_r.at[2 * s + c], relay_up, ang).start()

    def pass_on(s):
        for relay, dst, sems, d in ((relay_up, p2r, up_r, hi_design), (relay_down, qr, dn_r, lo_design)):
            @pl.when(slab == relay)
            def _():
                for c in range(2):
                    wait_bytes(rb.at[s, c], rl_r.at[2 * s + c])
                    send(rb.at[s, c], dst.at[s, c], rl_s, sems.at[s], d, ang).start()

    def h_new(s, z, top):
        ex, ey, ez = (E[s, c, z, E_ROWS] for c in range(3))
        if top:
            dzx, dzy = -ex, -ey
        else:
            dzx, dzy = E[s, 0, z + 1, E_ROWS] - ex, E[s, 1, z + 1, E_ROWS] - ey
        hx, hy, hz = (H[s, c, z + 1, H_ROWS] for c in range(3))
        hx = hx - 0.5 * ((next_y(ez) - ez) - dzy)
        hy = hy - 0.5 * (dzx - (E[s, 2, z, E_AHEAD] - ez))
        hz = hz - 0.5 * ((E[s, 1, z, E_AHEAD] - ey) - (next_y(ex) - ex))
        return hx, hy, hz

    def e_new(s, z, bottom):
        hx, hy, hz = (H[s, c, z + 1, H_ROWS] for c in range(3))
        if bottom:
            dzx, dzy = hx, hy
        else:
            dzx, dzy = hx - H[s, 0, z, H_ROWS], hy - H[s, 1, z, H_ROWS]
        kk = 0.5 * k[z]
        old = tuple(E[s, c, z, E_ROWS] for c in range(3))
        ex = old[0] + kk * ((hz - prev_y(hz)) - dzy)
        ey = old[1] + kk * (dzx - (hz - H[s, 2, z + 1, H_BEHIND]))
        ez = old[2] + kk * ((hy - H[s, 1, z + 1, H_BEHIND]) - (hx - prev_y(hx)))
        return old, (ex, ey, ez)

    def first_step(s):
        for z in range(NP):
            new = h_new(s, z, z == NP - 1)
            for c in range(3):
                H[s, c, z + 1, H_ROWS] = new[c]
        for c in range(2):
            p1s[s, c] = new[c]
        for z in range(NP):
            _, new = e_new(s, z, z == 0)
            for c in range(3):
                E[s, c, z, E_ROWS] = new[c]
                if z == 0 and c < 2:
                    qs[s, c] = new[c]
        new = h_new(s, NP - 1, True)
        for c in range(2):
            p2s[s, c] = new[c]

    edge = jnp.where(has_below, 0.5, 0.0).astype(F32)

    def fix_above(s):
        dx, dy = 0.5 * e0h[s, 1, H_ROWS], -0.5 * e0h[s, 0, H_ROWS]
        hx, hy = H[s, 0, NP, H_ROWS] + dx, H[s, 1, NP, H_ROWS] + dy
        H[s, 0, NP, H_ROWS] = hx
        H[s, 1, NP, H_ROWS] = hy
        k3 = 0.5 * k[NP - 1]
        E[s, 0, NP - 1, E_ROWS] = E[s, 0, NP - 1, E_ROWS] - k3 * dy
        E[s, 1, NP - 1, E_ROWS] = E[s, 1, NP - 1, E_ROWS] + k3 * dx
        E[s, 2, NP - 1, E_ROWS] = E[s, 2, NP - 1, E_ROWS] + k3 * (
            (dy + 0.5 * e0h[s, 0, H_BEHIND]) - (dx - prev_y(dx)))
        ku = 0.5 * epsu[...]
        E[s, 0, NP, E_ROWS] = qr[s, 0] + ku * hy
        E[s, 1, NP, E_ROWS] = qr[s, 1] - ku * hx

    def fix_below(s):
        dx, dy = edge * keep[s, 1, H_ROWS], -edge * keep[s, 0, H_ROWS]
        k0, kl = 0.5 * k[0], 0.5 * epsl[...]
        d = kl * ((dy + edge * keep[s, 0, H_BEHIND]) - (dx - prev_y(dx)))
        dz[E_ROWS] = d
        ex = E[s, 0, 0, E_ROWS] + k0 * (p1r[s, 1] + dy)
        ey = E[s, 1, 0, E_ROWS] - k0 * (p1r[s, 0] + dx)
        E[s, 0, 0, E_ROWS] = ex
        E[s, 1, 0, E_ROWS] = ey
        H[s, 0, 0, H_ROWS] = p2r[s, 0] + dx - 0.5 * (next_y(d) - d) + (edge * ey - 0.5 * kl * dx)
        H[s, 1, 0, H_ROWS] = p2r[s, 1] + dy + 0.5 * (dz[E_AHEAD] - d) - (edge * ex + 0.5 * kl * dy)

    def second_h(s, planes):
        for z in planes:
            new = h_new(s, z, False)
            for c in range(3):
                H[s, c, z + 1, H_ROWS] = new[c]
                fo[0, s, 1, c, z] = new[c]

    def second_e(s, planes):
        c0, s0, c1, s1 = (op(jnp.full((1, N), ph[t], F32)) for t in range(2) for op in (jnp.cos, jnp.sin))
        for z in planes:
            old, new = e_new(s, z, False)
            total = jnp.zeros((N, N), F32)
            for c in range(3):
                fo[0, s, 0, c, z] = new[c]
                re = so[0, s, 0, c, z] + old[c] * c0 + new[c] * c1
                im = so[0, s, 1, c, z] + old[c] * s0 + new[c] * s1
                so[0, s, 0, c, z] = re
                so[0, s, 1, c, z] = im
                if s == 1:
                    total = total + so[0, 0, 0, c, z] * re - so[0, 0, 1, c, z] * im
            if s == 1:
                dens[z] = total

    def lower_planes(s):
        @pl.when(has_below)
        def _():
            if s == 0:
                wait_bytes(epsl, up_r.at[2])
            wait_bytes(fo.at[0, s, 0, 0], up_r.at[s])

        fix_below(s)
        second_h(s, (0,))
        second_e(s, (0, 1))

    def upper_planes(s):
        @pl.when(has_above)
        def _():
            if s == 0:
                wait_bytes(epsu, dn_r.at[2])
            wait_bytes(fo.at[0, s, 0, 0], dn_r.at[s])

        fix_above(s)
        second_h(s, (2, 3))
        second_e(s, (2, 3))

    wait_bytes(so.at[0, 0], in_sem.at[0])
    load_eps.wait()
    first_step(0)
    incoming = (na - 1) + jnp.where(has_below, 1, 0) + jnp.where(has_above, 1, 0) + jnp.where(is_design, ns - 1, 0)
    incoming = incoming + jnp.where(jnp.logical_or(slab == relay_up, slab == relay_down), 1, 0)
    pl.semaphore_wait(bar, incoming)

    @pl.when(has_below)
    def _():
        down(ie.at[0], epsu, 2).start()
        for s in range(2):
            down(f.at[0, s, 0, 0:2, 0], e0h.at[s, :, H_ROWS], s).start()

    @pl.when(has_above)
    def _():
        up(ie.at[NP - 1], epsl, 2).start()
        up(p1s.at[0], p1r.at[0], 0).start()

    send_q(0)
    send_p2(0)
    wait_bytes(so.at[0, 1], in_sem.at[1])
    first_step(1)
    pl.when(has_above)(lambda: up(p1s.at[1], p1r.at[1], 1).start())
    send_q(1)
    send_p2(1)
    for s in range(2):
        pass_on(s)
    for s in range(2):
        second_h(s, (1,))
    fy[...] = filter_matrix(False).astype(jnp.bfloat16)
    mx[...] = (filter_matrix(True) * (0.5 / na)).astype(jnp.bfloat16)
    load_keep.wait()
    load_spectra.wait()

    def to_owner(part, side, owner):
        return send(gbuf.at[part, :, pl.ds(owner * cols, cols)], r1.at[part, pl.ds(side * HALF, HALF)],
                    g1_s, g1_r.at[part], owner, ang)

    def spread_density(part, first, side):
        planes = dens[first : first + HALF].reshape(HALF * N, N)
        along_y = sum(jnp.dot(p, fy[...], preferred_element_type=F32) for p in three_parts(planes))
        beside = jnp.concatenate([along_y[z * N : (z + 1) * N] for z in range(HALF)], axis=1)
        both = sum(jnp.dot(mx[...], p, preferred_element_type=F32) for p in three_parts(beside))
        for z in range(HALF):
            gbuf[part, z] = both[:, z * N : (z + 1) * N]
        d = (lo_design, hi_design)[side]
        for owner in range(ns):
            if owner != d:
                to_owner(part, side, owner).start()
        r1[part, side * HALF : (side + 1) * HALF] = gbuf[part, :, d * cols : (d + 1) * cols]

    second = (lower_planes, upper_planes)
    for odd in (0, 1):
        @pl.when(slab % 2 == odd)
        def _():
            design = (hi_design, lo_design)[odd]
            for part in (0, 1):
                upper = part if odd else 1 - part
                for s in range(2):
                    second[upper](s)
                pl.when(slab == design)(functools.partial(spread_density, part, HALF * upper, 1 - odd))

    for part in (0, 1):
        pl.when(is_design)(lambda: wait_bytes(r1.at[part, pl.ds(0, HALF)], g1_r.at[part]))
        pl.when(jnp.logical_not(is_design))(lambda: wait_bytes(r1.at[part], g1_r.at[part]))
        for j in range(1, na):
            send(r1.at[part], r2.at[part, ang], g2_s, g2_r.at[part], slab, lax.rem(ang + j, na)).start()
        r2[part, ang] = r1[part]
    for part in (0, 1):
        wait_bytes(r2.at[part, pl.ds(0, na - 1)], g2_r.at[part])
        total = r2[part, 0]
        for j in range(1, na):
            total = total + r2[part, j]
        if part == 0:
            g[0:HALF] = total[0:HALF]
            g[NP + HALF :] = total[HALF:]
        else:
            g[HALF : NP + HALF] = total

    wait_bytes(r2.at[:, pl.ds(0, na - 1)], g2_s)
    nine_planes = E.at[0, 0:3, 0:3, E_ROWS]
    pl.when(has_below)(lambda: wait_bytes(nine_planes, dn_s))
    pl.when(has_above)(lambda: wait_bytes(nine_planes, up_s))
    pl.when(jnp.logical_or(slab == relay_up, slab == relay_down))(lambda: wait_bytes(rb, rl_s))
    pl.when(is_design)(lambda: wait_bytes(gbuf.at[:, :, pl.ds(0, N - cols)], g1_s))


def write_out(a, b, c, x, y, z, sem):
    copies = [pltpu.make_async_copy(p, q, sem.at[i]) for i, (p, q) in enumerate(((a, x), (b, y), (c, z)))]
    for copy in copies:
        copy.start()
    for copy in copies:
        copy.wait()


def per_device(fields, spectra, inv_eps, step_phase):
    ns, na = lax.axis_size("slab"), lax.axis_size("angle")
    cols = N // ns
    shape = fields.shape
    vmem = pl.BlockSpec(memory_space=pltpu.VMEM)
    hbm = pl.BlockSpec(memory_space=pltpu.HBM)
    outs = (shape, shape, (2 * NP, cols, N))
    dma = pltpu.SemaphoreType.DMA
    planes = pltpu.VMEM((2, 2, N, N), F32)
    results = pl.pallas_call(
        functools.partial(kernel, ns, na),
        out_shape=[pltpu.VMEM(s, F32) for s in outs],
        in_specs=[hbm, hbm, hbm, pl.BlockSpec(memory_space=pltpu.SMEM)],
        out_specs=[vmem] * 3,
        scratch_shapes=[
            pltpu.VMEM((2, 3, NP + 1, PAD, N), F32),
            pltpu.VMEM((2, 3, NP + 1, PAD, N), F32),
            pltpu.VMEM((NP, N, N), F32),
            pltpu.VMEM((2, 2, PAD, N), F32),
            pltpu.VMEM((2, 2, PAD, N), F32),
            pltpu.VMEM((PAD, N), F32),
            planes, planes, planes, planes, planes, planes,
            pltpu.VMEM((N, N), F32),
            pltpu.VMEM((N, N), F32),
            pltpu.VMEM((NP, N, N), F32),
            pltpu.VMEM((N, N), jnp.bfloat16),
            pltpu.VMEM((N, N), jnp.bfloat16),
            pltpu.VMEM((2, HALF, N, N), F32),
            pltpu.VMEM((2, NP, cols, N), F32),
            pltpu.VMEM((2, na, NP, cols, N), F32),
            planes,
            dma((5,)), dma, dma((3,)), dma, dma((3,)), dma, dma((4,)), dma, dma((2,)), dma, dma((2,)),
        ],
        compiler_params=pltpu.CompilerParams(
            collective_id=0, has_side_effects=True, vmem_limit_bytes=48 * 2**20),
        name="steps",
    )(fields, spectra, inv_eps, step_phase)
    return tuple(pl.pallas_call(
        write_out,
        out_shape=[jax.ShapeDtypeStruct(s, F32) for s in outs],
        in_specs=[vmem] * 3,
        out_specs=[pl.BlockSpec(memory_space=pl.ANY)] * 3,
        scratch_shapes=[dma((3,))],
        compiler_params=pltpu.CompilerParams(has_side_effects=True, vmem_limit_bytes=2**20),
        name="write_out",
    )(*(pltpu.with_memory_space_constraint(r, pltpu.VMEM) for r in results)))


def solution(mesh):
    cells = P("angle", None, None, None, "slab", None, None)
    return jax.shard_map(
        per_device,
        mesh=mesh,
        in_specs=(cells, cells, P("slab", None, None), P()),
        out_specs=(cells, cells, P(None, "slab", None)),
        check_vma=False,
    )
```

time: 30.3 us -> 28.4 us (0.937)
  Pallas kernels: 29.6 us -> 27.6 us
    pallas_call x1, Pallas kernels: 26.8 us -> 24.9 us  [per_device(): pl.pallas_call(functools.partial(kernel, ns, na), out_shape=[pltpu.VMEM(s...]
where the time goes in v3:
time: 28.4 us; the launch traced here: 28.3 us
  Pallas kernels  27.6 us (97%)
  between operations  0.64 us (2%)
    pallas_call x1, Pallas kernels, per_device(): pl.pallas_call(functools.partial(kernel, ns, na), out_shape=[pltpu.VMEM(s...  24.9 us
    pallas_call x1, Pallas kernels, per_device(): pl.pallas_call(write_out, out_shape=[jax.ShapeDtypeStruct(s, F32) for s i...  2.73 us

profile of v3, /device:TPU:1, one launch (start us, length us, event | category | flops | bytes accessed | tf_op | source)
XLA Modules:
  0.0 28.3 jit_solution(14341081019592318522)
XLA Ops:
  0.6 24.9 %steps.1 = (f32[1,2,2,3,4,128,128]{6,5,4,3,2,1,0:T(8,128)S(1)}, f32[1,2,2,3,4,128,128]{6,5,4,3,2,1,0:T(8,128)S(1)}, f32[8,8,128]{2,1,0:T(8,128)S(1)}) custom-call(f32[1,2,2,3,4,128,128]{6,5,4,3,2,1,0:T(8,128)} %f.1, f32[1,2,2,3,4,128,128]{6,5,4,3,2,1,0:T(8,128)} %sp.1, f32[4,128,128]{2,1,0:T(8,128)} %ie.1, f32[2]{0:T(128)} %ph.1), custom_call_target="tpu_custom_call" | custom-call | tf_op jit(solution)/shard_map/steps/pallas_call | solution.py:371
  25.5 2.7 %write_out.1 = (f32[1,2,2,3,4,128,128]{6,5,4,3,2,1,0:T(8,128)}, f32[1,2,2,3,4,128,128]{6,5,4,3,2,1,0:T(8,128)}, f32[8,8,128]{2,1,0:T(8,128)}) custom-call(f32[1,2,2,3,4,128,128]{6,5,4,3,2,1,0:T(8,128)S(1)} %get-tuple-element.6.a, f32[1,2,2,3,4,128,128]{6,5,4,3,2,1,0:T(8,128)S(1)} %get-tuple-element.7.b, f32[8,8,128]{2,1,0:T(8,128)S(1)} %get-tuple-element.8.c), custom_call_target="tpu_custom_call" | custom-call | tf_op jit(solution)/shard_map/write_out/pallas_call | solution.py:399

commit v4 on v3

--- a/solution.py
+++ b/solution.py
@@ -14,6 +14,7 @@
 HALF = NP // 2
 PAD = 136
 TAPS = (0.375, 0.25, 0.0625)
+RELAYED = ((0, 0), (0, 1), (1, 1))
 E_ROWS, E_AHEAD = pl.ds(0, N), pl.ds(1, N)
 H_ROWS, H_BEHIND = pl.ds(8, N), pl.ds(7, N)
 
@@ -56,7 +57,7 @@
 
 def kernel(ns, na, f, sp, ie, ph, fo, so, g, E, H, k, e0h, keep, dz, p1s, p2s, qs, p1r, p2r, qr,
            epsu, epsl, dens, fy, mx, gbuf, r1, r2, rb, in_sem, dn_s, dn_r, up_s, up_r, rl_s, rl_r,
-           g1_s, g1_r, g2_s, g2_r):
+           g1_s, g1_r, g2_s, g2_r, ready):
     slab = lax.axis_index("slab")
     ang = lax.axis_index("angle")
     cols = N // ns
@@ -79,21 +80,30 @@
 
     pl.when(has_below)(lambda: signal(slab - 1, ang))
     pl.when(has_above)(lambda: signal(slab + 1, ang))
-    for d in (lo_design, hi_design):
-        pl.when(slab != d)(functools.partial(signal, d, ang))
-    pl.when(slab == hi_design)(lambda: signal(relay_up, ang))
-    pl.when(slab == lo_design)(lambda: signal(relay_down, ang))
-    for j in range(1, na):
-        signal(slab, lax.rem(ang + j, na))
-
+    pl.when(slab == relay_up)(lambda: signal(lo_design, ang))
+    pl.when(slab == relay_down)(lambda: signal(hi_design, ang))
+
+    @pl.when(is_design)
+    def _():
+        for d in range(ns):
+            if d not in (lo_design, hi_design):
+                signal(d, ang)
+        for j in range(1, na):
+            signal(jnp.where(slab == lo_design, lo_design - 1, hi_design + 1), lax.rem(ang + j, na))
+
+    @pl.when(jnp.logical_not(is_design))
+    def _():
+        for j in range(1, na):
+            signal(slab, lax.rem(ang + j, na))
+
+    load_keep = pltpu.make_async_copy(f.at[0, :, 0, 0:2, 0], keep.at[:, :, H_ROWS], in_sem.at[3])
+    load_keep.start()
     for s in range(2):
         pltpu.make_async_copy(f.at[0, s, 0], E.at[s, :, 0:NP, E_ROWS], in_sem.at[s]).start()
         pltpu.make_async_copy(f.at[0, s, 1], H.at[s, :, 1 : NP + 1, H_ROWS], in_sem.at[s]).start()
         if s == 0:
             load_eps = pltpu.make_async_copy(ie, k, in_sem.at[2])
             load_eps.start()
-    load_keep = pltpu.make_async_copy(f.at[0, :, 0, 0:2, 0], keep.at[:, :, H_ROWS], in_sem.at[3])
-    load_keep.start()
     load_spectra = pltpu.make_async_copy(sp, so, in_sem.at[4])
     load_spectra.start()
 
@@ -125,29 +135,32 @@
     def up(src, dst, i):
         return send(src, dst, up_s, up_r.at[i], slab + 1, ang)
 
-    def send_q(s):
-        pl.when(jnp.logical_and(has_below, slab != hi_design))(lambda: down(qs.at[s], qr.at[s], s).start())
-
-        @pl.when(slab == hi_design)
+    def send_outer(s, src, dst, neighbour, far, relay, exists, send_sem, recv_sem):
+        pl.when(jnp.logical_and(exists, slab != far))(
+            lambda: send(src.at[s], dst.at[s], send_sem, recv_sem.at[s], neighbour, ang).start())
+
+        @pl.when(slab == far)
         def _():
             for c in range(2):
-                send(qs.at[s, c], rb.at[s, c], dn_s, rl_r.at[2 * s + c], relay_down, ang).start()
+                if (s, c) in RELAYED:
+                    send(src.at[s, c], rb.at[RELAYED.index((s, c))], send_sem, rl_r.at[RELAYED.index((s, c))], relay, ang).start()
+            for c in range(2):
+                if (s, c) not in RELAYED:
+                    send(src.at[s, c], dst.at[s, c], send_sem, recv_sem.at[s], neighbour, ang).start()
+
+    def send_q(s):
+        send_outer(s, qs, qr, slab - 1, hi_design, relay_down, has_below, dn_s, dn_r)
 
     def send_p2(s):
-        pl.when(jnp.logical_and(has_above, slab != lo_design))(lambda: up(p2s.at[s], p2r.at[s], s).start())
-
-        @pl.when(slab == lo_design)
-        def _():
-            for c in range(2):
-                send(p2s.at[s, c], rb.at[s, c], up_s, rl_r.at[2 * s + c], relay_up, ang).start()
-
-    def pass_on(s):
+        send_outer(s, p2s, p2r, slab + 1, lo_design, relay_up, has_above, up_s, up_r)
+
+    def pass_on():
         for relay, dst, sems, d in ((relay_up, p2r, up_r, hi_design), (relay_down, qr, dn_r, lo_design)):
             @pl.when(slab == relay)
             def _():
-                for c in range(2):
-                    wait_bytes(rb.at[s, c], rl_r.at[2 * s + c])
-                    send(rb.at[s, c], dst.at[s, c], rl_s, sems.at[s], d, ang).start()
+                for i, (s, c) in enumerate(RELAYED):
+                    wait_bytes(rb.at[i], rl_r.at[i])
+                    send(rb.at[i], dst.at[s, c], rl_s, sems.at[s], d, ang).start()
 
     def h_new(s, z, top):
         ex, ey, ez = (E[s, c, z, E_ROWS] for c in range(3))
@@ -266,20 +279,27 @@
 
     wait_bytes(so.at[0, 0], in_sem.at[0])
     load_eps.wait()
+    load_keep.wait()
     first_step(0)
-    incoming = (na - 1) + jnp.where(has_below, 1, 0) + jnp.where(has_above, 1, 0) + jnp.where(is_design, ns - 1, 0)
-    incoming = incoming + jnp.where(jnp.logical_or(slab == relay_up, slab == relay_down), 1, 0)
+    incoming = jnp.where(has_below, 1, 0) + jnp.where(has_above, 1, 0)
+    incoming = incoming + jnp.where(is_design, 1, 2 + na - 1)
+    incoming = incoming + jnp.where(jnp.logical_or(slab == lo_design - 1, slab == hi_design + 1), na - 1, 0)
     pl.semaphore_wait(bar, incoming)
 
+    @pl.when(jnp.logical_not(is_design))
+    def _():
+        for d in (lo_design, hi_design):
+            pl.semaphore_signal(ready, inc=1, device_id=(d, ang), device_id_type=MESH)
+
     @pl.when(has_below)
     def _():
-        down(ie.at[0], epsu, 2).start()
+        down(k.at[0], epsu, 2).start()
         for s in range(2):
-            down(f.at[0, s, 0, 0:2, 0], e0h.at[s, :, H_ROWS], s).start()
+            down(keep.at[s, :, H_ROWS], e0h.at[s, :, H_ROWS], s).start()
 
     @pl.when(has_above)
     def _():
-        up(ie.at[NP - 1], epsl, 2).start()
+        up(k.at[NP - 1], epsl, 2).start()
         up(p1s.at[0], p1r.at[0], 0).start()
 
     send_q(0)
@@ -289,13 +309,11 @@
     pl.when(has_above)(lambda: up(p1s.at[1], p1r.at[1], 1).start())
     send_q(1)
     send_p2(1)
-    for s in range(2):
-        pass_on(s)
+    pass_on()
     for s in range(2):
         second_h(s, (1,))
     fy[...] = filter_matrix(False).astype(jnp.bfloat16)
     mx[...] = (filter_matrix(True) * (0.5 / na)).astype(jnp.bfloat16)
-    load_keep.wait()
     load_spectra.wait()
 
     def to_owner(part, side, owner):
@@ -315,16 +333,29 @@
                 to_owner(part, side, owner).start()
         r1[part, side * HALF : (side + 1) * HALF] = gbuf[part, :, d * cols : (d + 1) * cols]
 
-    second = (lower_planes, upper_planes)
-    for odd in (0, 1):
-        @pl.when(slab % 2 == odd)
-        def _():
-            design = (hi_design, lo_design)[odd]
-            for part in (0, 1):
-                upper = part if odd else 1 - part
+    def beside_core(planes_below):
+        for odd, planes in ((1, lower_planes), (0, upper_planes)):
+            @pl.when(slab % 2 == (odd if planes_below else 1 - odd))
+            def _():
                 for s in range(2):
-                    second[upper](s)
-                pl.when(slab == design)(functools.partial(spread_density, part, HALF * upper, 1 - odd))
+                    planes(s)
+
+    beside_core(True)
+    pl.when(is_design)(lambda: pl.semaphore_wait(ready, ns - 2))
+    for side, d in enumerate((lo_design, hi_design)):
+        pl.when(slab == d)(functools.partial(spread_density, 0, HALF * side, side))
+
+    @pl.when(slab == lo_design)
+    def _():
+        for s in range(2):
+            upper_planes(s)
+        spread_density(1, HALF, 0)
+
+    @pl.when(slab == hi_design)
+    def _():
+        for s in range(2):
+            lower_planes(s)
+        spread_density(1, 0, 1)
 
     for part in (0, 1):
         pl.when(is_design)(lambda: wait_bytes(r1.at[part, pl.ds(0, HALF)], g1_r.at[part]))
@@ -332,6 +363,9 @@
         for j in range(1, na):
             send(r1.at[part], r2.at[part, ang], g2_s, g2_r.at[part], slab, lax.rem(ang + j, na)).start()
         r2[part, ang] = r1[part]
+
+    pl.when(jnp.logical_not(is_design))(lambda: beside_core(False))
+
     for part in (0, 1):
         wait_bytes(r2.at[part, pl.ds(0, na - 1)], g2_r.at[part])
         total = r2[part, 0]
@@ -389,8 +423,9 @@
             pltpu.VMEM((2, HALF, N, N), F32),
             pltpu.VMEM((2, NP, cols, N), F32),
             pltpu.VMEM((2, na, NP, cols, N), F32),
-            planes,
-            dma((5,)), dma, dma((3,)), dma, dma((3,)), dma, dma((4,)), dma, dma((2,)), dma, dma((2,)),
+            pltpu.VMEM((len(RELAYED), N, N), F32),
+            dma((5,)), dma, dma((3,)), dma, dma((3,)), dma, dma((len(RELAYED),)), dma, dma((2,)), dma, dma((2,)),
+            pltpu.SemaphoreType.REGULAR,
         ],
         compiler_params=pltpu.CompilerParams(
             collective_id=0, has_side_effects=True, vmem_limit_bytes=48 * 2**20),

time: 28.4 us -> 27.3 us (0.961)
  Pallas kernels: 27.6 us -> 26.5 us
    pallas_call x1, Pallas kernels: 24.9 us -> 23.8 us  [per_device(): pl.pallas_call(functools.partial(kernel, ns, na), out_shape=[pltpu.VMEM(s...]
where the time goes in v4:
time: 27.3 us; the launch traced here: 27.2 us
  Pallas kernels  26.5 us (97%)
  between operations  0.64 us (2%)
    pallas_call x1, Pallas kernels, per_device(): pl.pallas_call(functools.partial(kernel, ns, na), out_shape=[pltpu.VMEM(s...  23.8 us
    pallas_call x1, Pallas kernels, per_device(): pl.pallas_call(write_out, out_shape=[jax.ShapeDtypeStruct(s, F32) for s i...  2.73 us

profile of v4, /device:TPU:1, one launch (start us, length us, event | category | flops | bytes accessed | tf_op | source)
XLA Modules:
  0.0 27.2 jit_solution(17801143481753080624)
XLA Ops:
  0.6 23.8 %steps.1 = (f32[1,2,2,3,4,128,128]{6,5,4,3,2,1,0:T(8,128)S(1)}, f32[1,2,2,3,4,128,128]{6,5,4,3,2,1,0:T(8,128)S(1)}, f32[8,8,128]{2,1,0:T(8,128)S(1)}) custom-call(f32[1,2,2,3,4,128,128]{6,5,4,3,2,1,0:T(8,128)} %f.1, f32[1,2,2,3,4,128,128]{6,5,4,3,2,1,0:T(8,128)} %sp.1, f32[4,128,128]{2,1,0:T(8,128)} %ie.1, f32[2]{0:T(128)} %ph.1), custom_call_target="tpu_custom_call" | custom-call | tf_op jit(solution)/shard_map/steps/pallas_call | solution.py:405
  24.4 2.7 %write_out.1 = (f32[1,2,2,3,4,128,128]{6,5,4,3,2,1,0:T(8,128)}, f32[1,2,2,3,4,128,128]{6,5,4,3,2,1,0:T(8,128)}, f32[8,8,128]{2,1,0:T(8,128)}) custom-call(f32[1,2,2,3,4,128,128]{6,5,4,3,2,1,0:T(8,128)S(1)} %get-tuple-element.6.a, f32[1,2,2,3,4,128,128]{6,5,4,3,2,1,0:T(8,128)S(1)} %get-tuple-element.7.b, f32[8,8,128]{2,1,0:T(8,128)S(1)} %get-tuple-element.8.c), custom_call_target="tpu_custom_call" | custom-call | tf_op jit(solution)/shard_map/write_out/pallas_call | solution.py:434

commit v5 on v4

--- a/solution.py
+++ b/solution.py
@@ -312,8 +312,8 @@
     pass_on()
     for s in range(2):
         second_h(s, (1,))
-    fy[...] = filter_matrix(False).astype(jnp.bfloat16)
-    mx[...] = (filter_matrix(True) * (0.5 / na)).astype(jnp.bfloat16)
+    fy[...] = jnp.concatenate([filter_matrix(False).astype(jnp.bfloat16)] * 3, axis=0)
+    mx[...] = jnp.concatenate([(filter_matrix(True) * (0.5 / na)).astype(jnp.bfloat16)] * 3, axis=1)
     load_spectra.wait()
 
     def to_owner(part, side, owner):
@@ -322,9 +322,9 @@
 
     def spread_density(part, first, side):
         planes = dens[first : first + HALF].reshape(HALF * N, N)
-        along_y = sum(jnp.dot(p, fy[...], preferred_element_type=F32) for p in three_parts(planes))
+        along_y = jnp.dot(jnp.concatenate(three_parts(planes), axis=1), fy[...], preferred_element_type=F32)
         beside = jnp.concatenate([along_y[z * N : (z + 1) * N] for z in range(HALF)], axis=1)
-        both = sum(jnp.dot(mx[...], p, preferred_element_type=F32) for p in three_parts(beside))
+        both = jnp.dot(mx[...], jnp.concatenate(three_parts(beside), axis=0), preferred_element_type=F32)
         for z in range(HALF):
             gbuf[part, z] = both[:, z * N : (z + 1) * N]
         d = (lo_design, hi_design)[side]
@@ -418,8 +418,8 @@
             pltpu.VMEM((N, N), F32),
             pltpu.VMEM((N, N), F32),
             pltpu.VMEM((NP, N, N), F32),
-            pltpu.VMEM((N, N), jnp.bfloat16),
-            pltpu.VMEM((N, N), jnp.bfloat16),
+            pltpu.VMEM((3 * N, N), jnp.bfloat16),
+            pltpu.VMEM((N, 3 * N), jnp.bfloat16),
             pltpu.VMEM((2, HALF, N, N), F32),
             pltpu.VMEM((2, NP, cols, N), F32),
             pltpu.VMEM((2, na, NP, cols, N), F32),

time: 27.3 us -> 27.2 us (level)
  no operation moved by 1% of the time
where the time goes in v5:
time: 27.2 us; the launch traced here: 27.1 us
  Pallas kernels  26.4 us (97%)
  between operations  0.64 us (2%)
    pallas_call x1, Pallas kernels, per_device(): pl.pallas_call(functools.partial(kernel, ns, na), out_shape=[pltpu.VMEM(s...  23.7 us
    pallas_call x1, Pallas kernels, per_device(): pl.pallas_call(write_out, out_shape=[jax.ShapeDtypeStruct(s, F32) for s i...  2.73 us

profile of v5, /device:TPU:1, one launch (start us, length us, event | category | flops | bytes accessed | tf_op | source)
XLA Modules:
  0.0 27.1 jit_solution(11702522962264736183)
XLA Ops:
  0.6 23.7 %steps.1 = (f32[1,2,2,3,4,128,128]{6,5,4,3,2,1,0:T(8,128)S(1)}, f32[1,2,2,3,4,128,128]{6,5,4,3,2,1,0:T(8,128)S(1)}, f32[8,8,128]{2,1,0:T(8,128)S(1)}) custom-call(f32[1,2,2,3,4,128,128]{6,5,4,3,2,1,0:T(8,128)} %f.1, f32[1,2,2,3,4,128,128]{6,5,4,3,2,1,0:T(8,128)} %sp.1, f32[4,128,128]{2,1,0:T(8,128)} %ie.1, f32[2]{0:T(128)} %ph.1), custom_call_target="tpu_custom_call" | custom-call | tf_op jit(solution)/shard_map/steps/pallas_call | solution.py:405
  24.4 2.7 %write_out.1 = (f32[1,2,2,3,4,128,128]{6,5,4,3,2,1,0:T(8,128)}, f32[1,2,2,3,4,128,128]{6,5,4,3,2,1,0:T(8,128)}, f32[8,8,128]{2,1,0:T(8,128)}) custom-call(f32[1,2,2,3,4,128,128]{6,5,4,3,2,1,0:T(8,128)S(1)} %get-tuple-element.6.a, f32[1,2,2,3,4,128,128]{6,5,4,3,2,1,0:T(8,128)S(1)} %get-tuple-element.7.b, f32[8,8,128]{2,1,0:T(8,128)S(1)} %get-tuple-element.8.c), custom_call_target="tpu_custom_call" | custom-call | tf_op jit(solution)/shard_map/write_out/pallas_call | solution.py:434

commit v6 on v5

--- a/solution.py
+++ b/solution.py
@@ -328,7 +328,7 @@
         for z in range(HALF):
             gbuf[part, z] = both[:, z * N : (z + 1) * N]
         d = (lo_design, hi_design)[side]
-        for owner in range(ns):
+        for owner in (*range(1, ns, 2), *range(0, ns, 2)):
             if owner != d:
                 to_owner(part, side, owner).start()
         r1[part, side * HALF : (side + 1) * HALF] = gbuf[part, :, d * cols : (d + 1) * cols]

time: 27.2 us -> 27.2 us (level)
  no operation moved by 1% of the time
where the time goes in v6:
time: 27.2 us; the launch traced here: 27 us
  Pallas kernels  26.3 us (97%)
  between operations  0.64 us (2%)
    pallas_call x1, Pallas kernels, per_device(): pl.pallas_call(functools.partial(kernel, ns, na), out_shape=[pltpu.VMEM(s...  23.6 us
    pallas_call x1, Pallas kernels, per_device(): pl.pallas_call(write_out, out_shape=[jax.ShapeDtypeStruct(s, F32) for s i...  2.73 us

profile of v6, /device:TPU:1, one launch (start us, length us, event | category | flops | bytes accessed | tf_op | source)
XLA Modules:
  0.0 27.0 jit_solution(12972956280910853547)
XLA Ops:
  0.6 23.6 %steps.1 = (f32[1,2,2,3,4,128,128]{6,5,4,3,2,1,0:T(8,128)S(1)}, f32[1,2,2,3,4,128,128]{6,5,4,3,2,1,0:T(8,128)S(1)}, f32[8,8,128]{2,1,0:T(8,128)S(1)}) custom-call(f32[1,2,2,3,4,128,128]{6,5,4,3,2,1,0:T(8,128)} %f.1, f32[1,2,2,3,4,128,128]{6,5,4,3,2,1,0:T(8,128)} %sp.1, f32[4,128,128]{2,1,0:T(8,128)} %ie.1, f32[2]{0:T(128)} %ph.1), custom_call_target="tpu_custom_call" | custom-call | tf_op jit(solution)/shard_map/steps/pallas_call | solution.py:405
  24.2 2.7 %write_out.1 = (f32[1,2,2,3,4,128,128]{6,5,4,3,2,1,0:T(8,128)}, f32[1,2,2,3,4,128,128]{6,5,4,3,2,1,0:T(8,128)}, f32[8,8,128]{2,1,0:T(8,128)}) custom-call(f32[1,2,2,3,4,128,128]{6,5,4,3,2,1,0:T(8,128)S(1)} %get-tuple-element.6.a, f32[1,2,2,3,4,128,128]{6,5,4,3,2,1,0:T(8,128)S(1)} %get-tuple-element.7.b, f32[8,8,128]{2,1,0:T(8,128)S(1)} %get-tuple-element.8.c), custom_call_target="tpu_custom_call" | custom-call | tf_op jit(solution)/shard_map/write_out/pallas_call | solution.py:434
